TPU v7x, 32 devices: a whole 2x2x4 slice. The times are simulated.
32 devices in a mesh: seq: 8 (over z, x), seg: 4 (over y, core).
Axes of the slice: x: 2, y: 2, z: 4, core: 2. Of those that a mesh axis runs over, the one named last changes fastest.
Arguments:
- tokens: bfloat16 [4, 2048, 1024], P('seg', 'seq'), may hold values from -6 to 6
- article_lengths: int32 [4, 8], P('seg'), may hold values from 1 to 2041, as said below
- gain_one: float32 [1024], replicated, may hold values from 0.1 to 1.9
- bias_one: float32 [1024], replicated, may hold values from -3 to 3
- w_qkv: bfloat16 [1024, 3072], P('seg'), may hold values from -0.25 to 0.25
- w_out: bfloat16 [1024, 1024], P('seg'), may hold values from -0.5 to 0.5
- gain_two: float32 [1024], replicated, may hold values from 0.1 to 1.9
- bias_two: float32 [1024], replicated, may hold values from -3 to 3
- w_up: bfloat16 [1024, 4096], P('seg'), may hold values from -0.1875 to 0.1875
- w_down: bfloat16 [4096, 1024], P('seg'), may hold values from -0.125 to 0.125
- cotangent: bfloat16 [4, 2048, 1024], P('seg', 'seq'), may hold values from -6 to 6
Outputs:
- result: bfloat16 [4, 2048, 1024], P('seg', 'seq')
- input_grad: float32 [4, 2048, 1024], P('seg', 'seq')
- grad_gain_one: float32 [1024], replicated
- grad_bias_one: float32 [1024], replicated
- grad_qkv: float32 [1024, 3072], P('seg', 'seq')
- grad_out: float32 [1024, 1024], P('seg', 'seq')
- grad_gain_two: float32 [1024], replicated
- grad_bias_two: float32 [1024], replicated
- grad_up: float32 [1024, 4096], P('seg', 'seq')
- grad_down: float32 [4096, 1024], P('seg', 'seq')
Inputs may be any that keep to these rules, and one draw needn't show every extreme that they name: `article_lengths`: each row holds 8 article lengths that sum to 2048; one of them, at a place drawn from the seed, exceeds 2048 - 256, the others are at most 32.
All inputs are finite; a program needn't handle non-finite values.
Results may differ from a plain program's by a relative error of at most 0.02.
Values may be sent and summed in bfloat16 or wider, within the bound.
A program may use at most 192 MiB of HBM per device.

v0:
```python
import math

import jax
import jax.numpy as jnp
from jax import lax
from jax.sharding import PartitionSpec as P

HEADS = 8
HEAD_DIM = 128


def passed_along(block, axis, distance):
    devices = range(lax.axis_size(axis))
    route = [(i - distance, i) for i in devices if i - distance in devices]
    return lax.ppermute(block, axis, route)


def shifted(value, axis, by):
    size = lax.axis_size(axis)
    return lax.ppermute(value, axis, [(i, (i + by) % size) for i in range(size)])


def layer_norm(values, gain, bias):
    center = values - jnp.mean(values, axis=-1, keepdims=True)
    spread = jnp.mean(center * center, axis=-1, keepdims=True)
    return center * lax.rsqrt(spread + 1e-05) * gain + bias


def smooth_act(values):
    return jax.nn.gelu(values, approximate=True)


def article_numbers(lengths_row, positions):
    bounds = jnp.cumsum(lengths_row)
    return jnp.sum((positions[:, None] >= bounds[None, :]).astype(jnp.int32), axis=1)


def per_device(
    tokens,
    article_lengths,
    gain_one,
    bias_one,
    w_qkv,
    w_out,
    gain_two,
    bias_two,
    w_up,
    w_down,
    cotangent,
):
    tok_rows = tokens.shape[1]
    model_width = tokens.shape[2]
    head_count = HEADS
    head_size = HEAD_DIM
    scale = 1.0 / math.sqrt(head_size)
    blocks_seq = lax.axis_size("seq")
    my_place = lax.axis_index("seq")
    full_qkv, full_out, full_up, full_down = (
        lax.all_gather(w_qkv, "seg", axis=0, tiled=True),
        lax.all_gather(w_out, "seg", axis=0, tiled=True),
        lax.all_gather(w_up, "seg", axis=0, tiled=True),
        lax.all_gather(w_down, "seg", axis=0, tiled=True),
    )
    inputs = tokens[0].astype(jnp.float32)
    normed, norm_one_back = jax.vjp(layer_norm, inputs, gain_one, bias_one)
    normed_low = normed.astype(jnp.bfloat16)
    projected = jnp.dot(normed_low, full_qkv, preferred_element_type=jnp.float32).astype(
        jnp.bfloat16
    )
    query_low = projected[:, :model_width]
    key_low = projected[:, model_width : 2 * model_width]
    value_low = projected[:, 2 * model_width :]
    query_heads = query_low.reshape(tok_rows, head_count, head_size)
    lengths_row = article_lengths[0]
    positions = my_place * tok_rows + jnp.arange(tok_rows, dtype=jnp.int32)
    query_art = article_numbers(lengths_row, positions)

    def scores_of(key_block, source):
        key_pos = source * tok_rows + jnp.arange(tok_rows, dtype=jnp.int32)
        key_art = article_numbers(lengths_row, key_pos)
        allowed = (key_pos[None, :] <= positions[:, None]) & (
            key_art[None, :] == query_art[:, None]
        )
        raw = (
            jnp.einsum(
                "qhd,khd->hqk",
                query_heads,
                key_block.reshape(tok_rows, head_count, head_size),
                preferred_element_type=jnp.float32,
            )
            * scale
        )
        return jnp.where(allowed[None], raw, -1e30)

    def forward_block(state, key_block, value_block, source):

        def forward_work(operands):
            (top, total, accum), key_now, value_now = operands
            scores = scores_of(key_now, source)
            new_top = jnp.maximum(top, jnp.max(scores, axis=2))
            factor = jnp.exp(top - new_top)
            weights = jnp.exp(scores - new_top[:, :, None])
            total = total * factor + jnp.sum(weights, axis=2)
            gathered = jnp.einsum(
                "hqk,khd->qhd",
                weights.astype(jnp.bfloat16),
                value_now.reshape(tok_rows, head_count, head_size),
                preferred_element_type=jnp.float32,
            ).reshape(tok_rows, model_width)
            accum = accum * jnp.repeat(factor.T, head_size, axis=1) + gathered
            return (new_top, total, accum)

        def forward_keep(operands):
            return operands[0]

        return lax.cond(
            source <= my_place, forward_work, forward_keep, (state, key_block, value_block)
        )

    start_state = (
        jnp.full((head_count, tok_rows), -1e30, jnp.float32),
        jnp.zeros((head_count, tok_rows), jnp.float32),
        jnp.zeros((tok_rows, model_width), jnp.float32),
    )
    state = forward_block(start_state, key_low, value_low, my_place)

    def forward_step(step, carry):
        key_block, value_block, state_now = carry
        key_block, value_block = passed_along((key_block, value_block), "seq", 1)
        source = (my_place - step) % blocks_seq
        return (key_block, value_block, forward_block(state_now, key_block, value_block, source))

    _, _, state = lax.fori_loop(1, blocks_seq, forward_step, (key_low, value_low, state))
    top, total, accum = state
    log_total = top + jnp.log(total)
    attended = accum / jnp.repeat(total.T, head_size, axis=1)
    attended_low = attended.astype(jnp.bfloat16)
    middle = inputs + jnp.dot(attended_low, full_out, preferred_element_type=jnp.float32)
    normed_two, norm_two_back = jax.vjp(layer_norm, middle, gain_two, bias_two)
    normed_two_low = normed_two.astype(jnp.bfloat16)
    hidden = jnp.dot(normed_two_low, full_up, preferred_element_type=jnp.float32)
    activated, act_back = jax.vjp(smooth_act, hidden)
    activated_low = activated.astype(jnp.bfloat16)
    outputs = middle + jnp.dot(activated_low, full_down, preferred_element_type=jnp.float32)
    result = outputs.astype(jnp.bfloat16)[None]
    grad_top = cotangent[0].astype(jnp.float32)
    grad_top_low = cotangent[0]
    grad_down = jnp.einsum(
        "tf,td->fd", activated_low, grad_top_low, preferred_element_type=jnp.float32
    )
    grad_act = jnp.einsum("td,fd->tf", grad_top_low, full_down, preferred_element_type=jnp.float32)
    (grad_hidden,) = act_back(grad_act)
    grad_hidden_low = grad_hidden.astype(jnp.bfloat16)
    grad_up = jnp.einsum(
        "td,tf->df", normed_two_low, grad_hidden_low, preferred_element_type=jnp.float32
    )
    grad_normed_two = jnp.einsum(
        "tf,df->td", grad_hidden_low, full_up, preferred_element_type=jnp.float32
    )
    grad_mid_norm, grad_gain_two, grad_bias_two = norm_two_back(grad_normed_two)
    grad_middle = grad_top + grad_mid_norm
    grad_middle_low = grad_middle.astype(jnp.bfloat16)
    grad_out = jnp.einsum(
        "tc,td->cd", attended_low, grad_middle_low, preferred_element_type=jnp.float32
    )
    grad_att = jnp.einsum(
        "td,cd->tc", grad_middle_low, full_out, preferred_element_type=jnp.float32
    )
    grad_att_low = grad_att.astype(jnp.bfloat16)
    grad_att_heads = grad_att_low.reshape(tok_rows, head_count, head_size)
    offsets = jnp.sum(
        (grad_att_low.astype(jnp.float32) * attended).reshape(tok_rows, head_count, head_size),
        axis=2,
    ).T

    def backward_block(operands, source):

        def backward_work(inner):
            grad_query, grad_key, grad_value, key_now, value_now = inner
            key_heads = key_now.reshape(tok_rows, head_count, head_size)
            value_heads = value_now.reshape(tok_rows, head_count, head_size)
            probs = jnp.exp(scores_of(key_now, source) - log_total[:, :, None])
            probs_low = probs.astype(jnp.bfloat16)
            grad_value = grad_value + jnp.einsum(
                "hqk,qhd->khd", probs_low, grad_att_heads, preferred_element_type=jnp.float32
            ).reshape(tok_rows, model_width)
            grad_probs = jnp.einsum(
                "qhd,khd->hqk", grad_att_heads, value_heads, preferred_element_type=jnp.float32
            )
            grad_scores = (probs * (grad_probs - offsets[:, :, None])).astype(jnp.bfloat16)
            grad_query = (
                grad_query
                + jnp.einsum(
                    "hqk,khd->qhd", grad_scores, key_heads, preferred_element_type=jnp.float32
                ).reshape(tok_rows, model_width)
                * scale
            )
            grad_key = (
                grad_key
                + jnp.einsum(
                    "hqk,qhd->khd", grad_scores, query_heads, preferred_element_type=jnp.float32
                ).reshape(tok_rows, model_width)
                * scale
            )
            return (grad_query, grad_key, grad_value, key_now, value_now)

        def backward_keep(inner):
            return inner

        return lax.cond(source <= my_place, backward_work, backward_keep, operands)

    def backward_step(step, carry):
        source = (my_place - step) % blocks_seq
        grad_query, grad_key, grad_value, key_block, value_block = backward_block(carry, source)
        key_block, value_block = passed_along((key_block, value_block), "seq", 1)
        grad_key, grad_value = (
            shifted(grad_key.astype(jnp.bfloat16), "seq", 1).astype(grad_key.dtype),
            shifted(grad_value.astype(jnp.bfloat16), "seq", 1).astype(grad_value.dtype),
        )
        return (grad_query, grad_key, grad_value, key_block, value_block)

    zero_rows = jnp.zeros((tok_rows, model_width), jnp.float32)
    grad_query, grad_key, grad_value, _, _ = lax.fori_loop(
        0, blocks_seq, backward_step, (zero_rows, zero_rows, zero_rows, key_low, value_low)
    )
    grad_proj_low = jnp.concatenate([grad_query, grad_key, grad_value], axis=1).astype(jnp.bfloat16)
    grad_qkv = jnp.einsum(
        "tc,tk->ck", normed_low, grad_proj_low, preferred_element_type=jnp.float32
    )
    grad_normed = jnp.einsum(
        "tk,ck->tc", grad_proj_low, full_qkv, preferred_element_type=jnp.float32
    )
    grad_in_norm, grad_gain_one, grad_bias_one = norm_one_back(grad_normed)
    input_grad = (grad_middle + grad_in_norm)[None]
    part_qkv, part_out, part_up, part_down = (
        lax.psum_scatter(
            grad_qkv.astype(jnp.bfloat16), "seg", scatter_dimension=0, tiled=True
        ).astype(jnp.float32),
        lax.psum_scatter(
            grad_out.astype(jnp.bfloat16), "seg", scatter_dimension=0, tiled=True
        ).astype(jnp.float32),
        lax.psum_scatter(
            grad_up.astype(jnp.bfloat16), "seg", scatter_dimension=0, tiled=True
        ).astype(jnp.float32),
        lax.psum_scatter(
            grad_down.astype(jnp.bfloat16), "seg", scatter_dimension=0, tiled=True
        ).astype(jnp.float32),
    )
    sum_qkv, sum_out, sum_up, sum_down = (
        lax.psum_scatter(
            part_qkv.astype(jnp.bfloat16), "seq", scatter_dimension=1, tiled=True
        ).astype(jnp.float32),
        lax.psum_scatter(
            part_out.astype(jnp.bfloat16), "seq", scatter_dimension=1, tiled=True
        ).astype(jnp.float32),
        lax.psum_scatter(
            part_up.astype(jnp.bfloat16), "seq", scatter_dimension=1, tiled=True
        ).astype(jnp.float32),
        lax.psum_scatter(
            part_down.astype(jnp.bfloat16), "seq", scatter_dimension=1, tiled=True
        ).astype(jnp.float32),
    )
    sum_gain_one, sum_bias_one, sum_gain_two, sum_bias_two = lax.psum(
        (grad_gain_one, grad_bias_one, grad_gain_two, grad_bias_two), ("seq", "seg")
    )
    return (
        result,
        input_grad,
        sum_gain_one,
        sum_bias_one,
        sum_qkv,
        sum_out,
        sum_gain_two,
        sum_bias_two,
        sum_up,
        sum_down,
    )


def solution(mesh):
    return jax.shard_map(
        per_device,
        mesh=mesh,
        in_specs=(
            P("seg", "seq", None),
            P("seg", None),
            P(),
            P(),
            P("seg", None),
            P("seg", None),
            P(),
            P(),
            P("seg", None),
            P("seg", None),
            P("seg", "seq", None),
        ),
        out_specs=(
            P("seg", "seq", None),
            P("seg", "seq", None),
            P(),
            P(),
            P("seg", "seq"),
            P("seg", "seq"),
            P(),
            P(),
            P("seg", "seq"),
            P("seg", "seq"),
        ),
        check_vma=False,
    )
```

profile of v0, /device:TPU:4, one launch (start us, length us, event | category | flops | bytes accessed | tf_op | source)
XLA Modules:
  0.0 1207.6 jit_solution(9451645278836505428)
XLA Ops:
  11.0 45.1 %all-gather.5.cloned.1.call-done = bf16[1024,3072]{1,0:T(8,128)(2,1)} async-done(((bf16[256,3072]{1,0:T(8,128)(2,1)}), bf16[1024,3072]{1,0:T(8,128)(2,1)}) %all-gather.5.cloned.1.call-update) | async-done | bytes 6291472 | tf_op jit(solution)/shard_map/all_gather | solution.py:59
  65.6 193.5 %while.48 = (s32[]{:T(128)}, bf16[256,1024]{1,0:T(8,128)(2,1)}, bf16[256,1024]{0,1:T(8,128)(2,1)S(1)}, f32[8,256]{1,0:T(8,128)S(1)}, f32[8,256]{1,0:T(8,128)S(1)...) while((s32[]{:T(128)}, bf16[256,1024]{1,0:T(8,128)(2,1)}, ...), condition=%wide.region_13.14_spmd.clone, body=%wide.region_6.13_spmd.clone.sunk | while | flops 274936128 | bytes 20851336 | solution.py:133
  74.0 9.1 collective-permute-done
  83.1 10.6 collective-permute-done.1
  95.3 6.7 collective-permute-start
  106.4 8.3 collective-permute-done
  114.7 9.6 collective-permute-done.1
  130.3 7.6 collective-permute-start.1
  142.9 8.8 collective-permute-done.1
  153.4 7.5 collective-permute-start
  166.1 7.4 collective-permute-done
  173.6 7.8 collective-permute-done.1
  193.5 7.4 collective-permute-done
  200.9 6.9 collective-permute-done.1
  219.8 7.4 collective-permute-done
  240.1 6.4 collective-permute-start.1
  264.4 7.9 fusion.76
  272.3 11.5 fusion.29
  301.7 391.9 %while.49 = (s32[]{:T(128)}, f32[256,1024]{0,1:T(8,128)}, f32[256,1024]{0,1:T(8,128)}, f32[256,1024]{0,1:T(8,128)}, bf16[256,1024]{0,1:T(8,128)(2,1)S(1)}, /*ind...) while((s32[]{:T(128)}, f32[256,1024]{0,1:T(8,128)}, ...), condition=%wide.region_24.25_spmd.clone, body=%wide.region_19.24_spmd.clone.sunk | while | flops 677845312 | bytes 65694592 | solution.py:223
  303.8 7.3 conditional.7
  330.8 10.6 collective-permute-done.2
  358.0 10.6 collective-permute-start.2
  384.5 7.9 collective-permute-done.2
  414.1 12.3 %collective-permute-start.3 = (bf16[256,1024]{0,1:T(8,128)(2,1)}, bf16[256,1024]{0,1:T(8,128)(2,1)S(1)}, u32[]{:S(2)}, u32[]{:S(2)}) collective-permute-start(bf16[256,1024]{0,1:T(8,128)(2,1)} %convert_element_type.271), channel_id=1, source_target_pairs={{0,4},{4,8},{8,12},{12,16},{16,20},{20,24},{24,28},{28,0},{1,5},{5... | collective-permute-start | bytes 1572872 | tf_op jit(solution)/shard_map/while/body/eval_jaxpr/ppermute | solution.py:20
  456.8 11.4 collective-permute-start.2
  472.3 10.9 collective-permute-start.4
  506.9 8.0 collective-permute-start.2
  515.8 8.0 collective-permute-start.3
  528.1 10.9 collective-permute-start.5
  562.0 7.4 collective-permute-start.3
  569.5 10.1 collective-permute-start.4
  595.4 6.5 collective-permute-done.5
  604.7 6.5 collective-permute-start.2
  616.6 8.7 collective-permute-start.4
  643.0 7.9 collective-permute-done.5
  663.2 7.2 collective-permute-start.4
  675.8 7.3 collective-permute-done.2
  703.1 8.4 convolution_convert_fusion
  712.7 7.3 convolution_convert_fusion.1
  722.3 51.9 %reduce-scatter.15.cloned.1.call-done = bf16[256,3072]{1,0:T(8,128)(2,1)} async-done(((bf16[1024,3072]{1,0:T(8,128)(2,1)}), bf16[256,3072]{1,0:T(8,128)(2,1)}) %reduce-scatter.15.cloned.1.call-update) | async-done | bytes 1572880 | tf_op jit(solution)/shard_map/reduce_scatter | solution.py:236
  777.1 71.5 %reduce-scatter.23.cloned.1.call-done = bf16[1024,1024]{1,0:T(8,128)(2,1)} async-done(((bf16[4096,1024]{1,0:T(8,128)(2,1)}), bf16[1024,1024]{1,0:T(8,128)(2,1)}) %reduce-scatter.23.cloned.1.call-update) | async-done | bytes 2097168 | tf_op jit(solution)/shard_map/reduce_scatter | solution.py:245
  852.6 70.5 %reduce-scatter.19.cloned.1.call-done = bf16[256,4096]{1,0:T(8,128)(2,1)} async-done(((bf16[1024,4096]{1,0:T(8,128)(2,1)}), bf16[256,4096]{1,0:T(8,128)(2,1)}) %reduce-scatter.19.cloned.1.call-update) | async-done | bytes 2097168 | tf_op jit(solution)/shard_map/reduce_scatter | solution.py:242
  929.6 42.3 %all-reduce = (f32[1024]{0:T(1024)}, f32[1024]{0:T(1024)}, f32[1024]{0:T(1024)}, f32[1024]{0:T(1024)}) all-reduce(f32[1024]{0:T(1024)S(1)} %get-tuple-element.885, f32[1024]{0:T(1024)S(1)} %get-tuple-element.888, f32[1024]{0:T(1024)S(1)} %get-tuple-element.883, ...), channel_id=1, replica_groups=mesh['seq'=8,'seg'=4] {'seq','seg'}, use_global_device_ids=true, to_apply=%region_28.29 | all-reduce | flops 4096 | bytes 32768 | tf_op jit(solution)/shard_map/psum | solution.py:263
  974.7 7.0 fusion.40
  981.6 8.5 reduce-scatter.27.cloned.1.call-done
  991.7 66.0 %reduce-scatter.25.cloned.1.call-done = bf16[384,256]{1,0:T(8,128)(2,1)} async-done(((bf16[3072,256]{1,0:T(8,128)(2,1)}), bf16[384,256]{1,0:T(8,128)(2,1)}) %reduce-scatter.25.cloned.1.call-update) | async-done | bytes 196624
  1059.6 68.3 %reduce-scatter.29.cloned.1.call-done = bf16[128,1024]{1,0:T(8,128)(2,1)} async-done(((bf16[1024,1024]{1,0:T(8,128)(2,1)}), bf16[128,1024]{1,0:T(8,128)(2,1)}) %reduce-scatter.29.cloned.1.call-update) | async-done | bytes 262160
  1129.9 68.8 %reduce-scatter.21.cloned.1.call-done = bf16[256,512]{1,0:T(8,128)(2,1)} async-done(((bf16[256,4096]{1,0:T(8,128)(2,1)}), bf16[256,512]{1,0:T(8,128)(2,1)}) %reduce-scatter.21.cloned.1.call-update) | async-done | bytes 262160 | tf_op jit(solution)/shard_map/reduce_scatter | solution.py:256
  (371 shorter events, 391.9 us)
Async XLA Ops:
  7.2 48.9 %all-gather.5.cloned.1.call-start = ((), (), s32[]{:S(2)}) async-start(), calls=%async_computation.8 | async-start | bytes 7864320 | tf_op jit(solution)/shard_map/all_gather | solution.py:59
  7.9 252.7 %all-gather.7.cloned.1.call-start = ((), (), s32[]{:S(2)}) async-start(), calls=%async_computation.9 | async-start | bytes 2621440 | tf_op jit(solution)/shard_map/all_gather | solution.py:60
  8.7 255.7 %all-gather.9.cloned.1.call-start = ((), (), s32[]{:S(2)}) async-start(), calls=%async_computation.10 | async-start | bytes 10485760 | tf_op jit(solution)/shard_map/all_gather | solution.py:61
  9.4 262.9 %all-gather.11.cloned.1.call-start = ((), (), s32[]{:S(2)}) async-start(), calls=%async_computation.11 | async-start | bytes 10485760 | tf_op jit(solution)/shard_map/all_gather | solution.py:62
  10.0 710.1 %reduce-scatter.17.cloned.1.call-start = ((), (), s32[]{:S(2)}) async-start(), calls=%async_computation.13 | async-start | bytes 2621440 | tf_op jit(solution)/shard_map/reduce_scatter | solution.py:239
  70.6 23.1 %collective-permute-start.1 = (bf16[256,1024]{0,1:T(8,128)(2,1)}, bf16[256,1024]{0,1:T(8,128)(2,1)S(1)}, u32[]{:S(2)}, u32[]{:S(2)}) collective-permute-start(bf16[256,1024]{0,1:T(8,128)(2,1)} %copy-done.20), channel_id=1, source_target_pairs={{0,4},{4,8},{8,12},{12,16},{16,20},{20,24},{24,28},{1,5},{5,9},{9,... | collective-permute-start | bytes 1572872 | tf_op jit(solution)/shard_map/while/body/eval_jaxpr/ppermute | solution.py:15
  102.0 22.3 %collective-permute-start.1 = (bf16[256,1024]{0,1:T(8,128)(2,1)}, bf16[256,1024]{0,1:T(8,128)(2,1)S(1)}, u32[]{:S(2)}, u32[]{:S(2)}) collective-permute-start(bf16[256,1024]{0,1:T(8,128)(2,1)} %copy-done.20), channel_id=1, source_target_pairs={{0,4},{4,8},{8,12},{12,16},{16,20},{20,24},{24,28},{1,5},{5,9},{9,... | collective-permute-start | bytes 1572872 | tf_op jit(solution)/shard_map/while/body/eval_jaxpr/ppermute | solution.py:15
  130.3 21.5 %collective-permute-start.1 = (bf16[256,1024]{0,1:T(8,128)(2,1)}, bf16[256,1024]{0,1:T(8,128)(2,1)S(1)}, u32[]{:S(2)}, u32[]{:S(2)}) collective-permute-start(bf16[256,1024]{0,1:T(8,128)(2,1)} %copy-done.20), channel_id=1, source_target_pairs={{0,4},{4,8},{8,12},{12,16},{16,20},{20,24},{24,28},{1,5},{5,9},{9,... | collective-permute-start | bytes 1572872 | tf_op jit(solution)/shard_map/while/body/eval_jaxpr/ppermute | solution.py:15
  160.9 20.5 %collective-permute-start.1 = (bf16[256,1024]{0,1:T(8,128)(2,1)}, bf16[256,1024]{0,1:T(8,128)(2,1)S(1)}, u32[]{:S(2)}, u32[]{:S(2)}) collective-permute-start(bf16[256,1024]{0,1:T(8,128)(2,1)} %copy-done.20), channel_id=1, source_target_pairs={{0,4},{4,8},{8,12},{12,16},{16,20},{20,24},{24,28},{1,5},{5,9},{9,... | collective-permute-start | bytes 1572872 | tf_op jit(solution)/shard_map/while/body/eval_jaxpr/ppermute | solution.py:15
  291.0 483.3 %reduce-scatter.15.cloned.1.call-start = ((), (), s32[]{:S(2)}) async-start(), calls=%async_computation.12 | async-start | bytes 7864320 | tf_op jit(solution)/shard_map/reduce_scatter | solution.py:236
  312.0 29.4 %collective-permute-start.2 = (bf16[256,1024]{0,1:T(8,128)(2,1)}, bf16[256,1024]{0,1:T(8,128)(2,1)S(1)}, u32[]{:S(2)}, u32[]{:S(2)}) collective-permute-start(bf16[256,1024]{0,1:T(8,128)(2,1)} %convert_element_type.269), channel_id=1, source_target_pairs={{0,4},{4,8},{8,12},{12,16},{16,20},{20,24},{24,28},{28,0},{1,5},{5... | collective-permute-start | bytes 1572872 | tf_op jit(solution)/shard_map/while/body/eval_jaxpr/ppermute | solution.py:20
  317.1 30.0 %collective-permute-start.3 = (bf16[256,1024]{0,1:T(8,128)(2,1)}, bf16[256,1024]{0,1:T(8,128)(2,1)S(1)}, u32[]{:S(2)}, u32[]{:S(2)}) collective-permute-start(bf16[256,1024]{0,1:T(8,128)(2,1)} %convert_element_type.271), channel_id=1, source_target_pairs={{0,4},{4,8},{8,12},{12,16},{16,20},{20,24},{24,28},{28,0},{1,5},{5... | collective-permute-start | bytes 1572872 | tf_op jit(solution)/shard_map/while/body/eval_jaxpr/ppermute | solution.py:20
  320.4 29.2 %collective-permute-start.4 = (bf16[256,1024]{0,1:T(8,128)(2,1)S(1)}, bf16[256,1024]{0,1:T(8,128)(2,1)S(1)}, u32[]{:S(2)}, u32[]{:S(2)}) collective-permute-start(bf16[256,1024]{0,1:T(8,128)(2,1)S(1)} %copy.166), channel_id=1, source_target_pairs={{0,4},{4,8},{8,12},{12,16},{16,20},{20,24},{24,28},{1,5},{5,9},{9,... | collective-permute-start | bytes 1572872 | tf_op jit(solution)/shard_map/while/body/eval_jaxpr/ppermute | solution.py:15
  325.5 29.8 %collective-permute-start.5 = (bf16[256,1024]{1,0:T(8,128)(2,1)}, bf16[256,1024]{1,0:T(8,128)(2,1)S(1)}, u32[]{:S(2)}, u32[]{:S(2)}) collective-permute-start(bf16[256,1024]{1,0:T(8,128)(2,1)} %copy.167), channel_id=1, source_target_pairs={{0,4},{4,8},{8,12},{12,16},{16,20},{20,24},{24,28},{1,5},{5,9},{9,... | collective-permute-start | bytes 1572872 | tf_op jit(solution)/shard_map/while/body/eval_jaxpr/ppermute | solution.py:15
  358.0 34.3 %collective-permute-start.2 = (bf16[256,1024]{0,1:T(8,128)(2,1)}, bf16[256,1024]{0,1:T(8,128)(2,1)S(1)}, u32[]{:S(2)}, u32[]{:S(2)}) collective-permute-start(bf16[256,1024]{0,1:T(8,128)(2,1)} %convert_element_type.269), channel_id=1, source_target_pairs={{0,4},{4,8},{8,12},{12,16},{16,20},{20,24},{24,28},{28,0},{1,5},{5... | collective-permute-start | bytes 1572872 | tf_op jit(solution)/shard_map/while/body/eval_jaxpr/ppermute | solution.py:20
  369.5 28.5 %collective-permute-start.3 = (bf16[256,1024]{0,1:T(8,128)(2,1)}, bf16[256,1024]{0,1:T(8,128)(2,1)S(1)}, u32[]{:S(2)}, u32[]{:S(2)}) collective-permute-start(bf16[256,1024]{0,1:T(8,128)(2,1)} %convert_element_type.271), channel_id=1, source_target_pairs={{0,4},{4,8},{8,12},{12,16},{16,20},{20,24},{24,28},{28,0},{1,5},{5... | collective-permute-start | bytes 1572872 | tf_op jit(solution)/shard_map/while/body/eval_jaxpr/ppermute | solution.py:20
  372.8 28.3 %collective-permute-start.4 = (bf16[256,1024]{0,1:T(8,128)(2,1)S(1)}, bf16[256,1024]{0,1:T(8,128)(2,1)S(1)}, u32[]{:S(2)}, u32[]{:S(2)}) collective-permute-start(bf16[256,1024]{0,1:T(8,128)(2,1)S(1)} %copy.166), channel_id=1, source_target_pairs={{0,4},{4,8},{8,12},{12,16},{16,20},{20,24},{24,28},{1,5},{5,9},{9,... | collective-permute-start | bytes 1572872 | tf_op jit(solution)/shard_map/while/body/eval_jaxpr/ppermute | solution.py:15
  379.1 28.3 %collective-permute-start.5 = (bf16[256,1024]{1,0:T(8,128)(2,1)}, bf16[256,1024]{1,0:T(8,128)(2,1)S(1)}, u32[]{:S(2)}, u32[]{:S(2)}) collective-permute-start(bf16[256,1024]{1,0:T(8,128)(2,1)} %copy.167), channel_id=1, source_target_pairs={{0,4},{4,8},{8,12},{12,16},{16,20},{20,24},{24,28},{1,5},{5,9},{9,... | collective-permute-start | bytes 1572872 | tf_op jit(solution)/shard_map/while/body/eval_jaxpr/ppermute | solution.py:15
  410.2 32.3 %collective-permute-start.2 = (bf16[256,1024]{0,1:T(8,128)(2,1)}, bf16[256,1024]{0,1:T(8,128)(2,1)S(1)}, u32[]{:S(2)}, u32[]{:S(2)}) collective-permute-start(bf16[256,1024]{0,1:T(8,128)(2,1)} %convert_element_type.269), channel_id=1, source_target_pairs={{0,4},{4,8},{8,12},{12,16},{16,20},{20,24},{24,28},{28,0},{1,5},{5... | collective-permute-start | bytes 1572872 | tf_op jit(solution)/shard_map/while/body/eval_jaxpr/ppermute | solution.py:20
  414.1 33.9 %collective-permute-start.3 = (bf16[256,1024]{0,1:T(8,128)(2,1)}, bf16[256,1024]{0,1:T(8,128)(2,1)S(1)}, u32[]{:S(2)}, u32[]{:S(2)}) collective-permute-start(bf16[256,1024]{0,1:T(8,128)(2,1)} %convert_element_type.271), channel_id=1, source_target_pairs={{0,4},{4,8},{8,12},{12,16},{16,20},{20,24},{24,28},{28,0},{1,5},{5... | collective-permute-start | bytes 1572872 | tf_op jit(solution)/shard_map/while/body/eval_jaxpr/ppermute | solution.py:20
  426.5 22.7 %collective-permute-start.4 = (bf16[256,1024]{0,1:T(8,128)(2,1)S(1)}, bf16[256,1024]{0,1:T(8,128)(2,1)S(1)}, u32[]{:S(2)}, u32[]{:S(2)}) collective-permute-start(bf16[256,1024]{0,1:T(8,128)(2,1)S(1)} %copy.166), channel_id=1, source_target_pairs={{0,4},{4,8},{8,12},{12,16},{16,20},{20,24},{24,28},{1,5},{5,9},{9,... | collective-permute-start | bytes 1572872 | tf_op jit(solution)/shard_map/while/body/eval_jaxpr/ppermute | solution.py:15
  431.7 22.3 %collective-permute-start.5 = (bf16[256,1024]{1,0:T(8,128)(2,1)}, bf16[256,1024]{1,0:T(8,128)(2,1)S(1)}, u32[]{:S(2)}, u32[]{:S(2)}) collective-permute-start(bf16[256,1024]{1,0:T(8,128)(2,1)} %copy.167), channel_id=1, source_target_pairs={{0,4},{4,8},{8,12},{12,16},{16,20},{20,24},{24,28},{1,5},{5,9},{9,... | collective-permute-start | bytes 1572872 | tf_op jit(solution)/shard_map/while/body/eval_jaxpr/ppermute | solution.py:15
  456.8 34.8 %collective-permute-start.2 = (bf16[256,1024]{0,1:T(8,128)(2,1)}, bf16[256,1024]{0,1:T(8,128)(2,1)S(1)}, u32[]{:S(2)}, u32[]{:S(2)}) collective-permute-start(bf16[256,1024]{0,1:T(8,128)(2,1)} %convert_element_type.269), channel_id=1, source_target_pairs={{0,4},{4,8},{8,12},{12,16},{16,20},{20,24},{24,28},{28,0},{1,5},{5... | collective-permute-start | bytes 1572872 | tf_op jit(solution)/shard_map/while/body/eval_jaxpr/ppermute | solution.py:20
  469.0 28.2 %collective-permute-start.3 = (bf16[256,1024]{0,1:T(8,128)(2,1)}, bf16[256,1024]{0,1:T(8,128)(2,1)S(1)}, u32[]{:S(2)}, u32[]{:S(2)}) collective-permute-start(bf16[256,1024]{0,1:T(8,128)(2,1)} %convert_element_type.271), channel_id=1, source_target_pairs={{0,4},{4,8},{8,12},{12,16},{16,20},{20,24},{24,28},{28,0},{1,5},{5... | collective-permute-start | bytes 1572872 | tf_op jit(solution)/shard_map/while/body/eval_jaxpr/ppermute | solution.py:20
  472.3 26.1 %collective-permute-start.4 = (bf16[256,1024]{0,1:T(8,128)(2,1)S(1)}, bf16[256,1024]{0,1:T(8,128)(2,1)S(1)}, u32[]{:S(2)}, u32[]{:S(2)}) collective-permute-start(bf16[256,1024]{0,1:T(8,128)(2,1)S(1)} %copy.166), channel_id=1, source_target_pairs={{0,4},{4,8},{8,12},{12,16},{16,20},{20,24},{24,28},{1,5},{5,9},{9,... | collective-permute-start | bytes 1572872 | tf_op jit(solution)/shard_map/while/body/eval_jaxpr/ppermute | solution.py:15
  483.2 20.9 %collective-permute-start.5 = (bf16[256,1024]{1,0:T(8,128)(2,1)}, bf16[256,1024]{1,0:T(8,128)(2,1)S(1)}, u32[]{:S(2)}, u32[]{:S(2)}) collective-permute-start(bf16[256,1024]{1,0:T(8,128)(2,1)} %copy.167), channel_id=1, source_target_pairs={{0,4},{4,8},{8,12},{12,16},{16,20},{20,24},{24,28},{1,5},{5,9},{9,... | collective-permute-start | bytes 1572872 | tf_op jit(solution)/shard_map/while/body/eval_jaxpr/ppermute | solution.py:15
  506.9 33.3 %collective-permute-start.2 = (bf16[256,1024]{0,1:T(8,128)(2,1)}, bf16[256,1024]{0,1:T(8,128)(2,1)S(1)}, u32[]{:S(2)}, u32[]{:S(2)}) collective-permute-start(bf16[256,1024]{0,1:T(8,128)(2,1)} %convert_element_type.269), channel_id=1, source_target_pairs={{0,4},{4,8},{8,12},{12,16},{16,20},{20,24},{24,28},{28,0},{1,5},{5... | collective-permute-start | bytes 1572872 | tf_op jit(solution)/shard_map/while/body/eval_jaxpr/ppermute | solution.py:20
  515.8 30.1 %collective-permute-start.3 = (bf16[256,1024]{0,1:T(8,128)(2,1)}, bf16[256,1024]{0,1:T(8,128)(2,1)S(1)}, u32[]{:S(2)}, u32[]{:S(2)}) collective-permute-start(bf16[256,1024]{0,1:T(8,128)(2,1)} %convert_element_type.271), channel_id=1, source_target_pairs={{0,4},{4,8},{8,12},{12,16},{16,20},{20,24},{24,28},{28,0},{1,5},{5... | collective-permute-start | bytes 1572872 | tf_op jit(solution)/shard_map/while/body/eval_jaxpr/ppermute | solution.py:20
  523.8 25.6 %collective-permute-start.4 = (bf16[256,1024]{0,1:T(8,128)(2,1)S(1)}, bf16[256,1024]{0,1:T(8,128)(2,1)S(1)}, u32[]{:S(2)}, u32[]{:S(2)}) collective-permute-start(bf16[256,1024]{0,1:T(8,128)(2,1)S(1)} %copy.166), channel_id=1, source_target_pairs={{0,4},{4,8},{8,12},{12,16},{16,20},{20,24},{24,28},{1,5},{5,9},{9,... | collective-permute-start | bytes 1572872 | tf_op jit(solution)/shard_map/while/body/eval_jaxpr/ppermute | solution.py:15
  528.1 27.5 %collective-permute-start.5 = (bf16[256,1024]{1,0:T(8,128)(2,1)}, bf16[256,1024]{1,0:T(8,128)(2,1)S(1)}, u32[]{:S(2)}, u32[]{:S(2)}) collective-permute-start(bf16[256,1024]{1,0:T(8,128)(2,1)} %copy.167), channel_id=1, source_target_pairs={{0,4},{4,8},{8,12},{12,16},{16,20},{20,24},{24,28},{1,5},{5,9},{9,... | collective-permute-start | bytes 1572872 | tf_op jit(solution)/shard_map/while/body/eval_jaxpr/ppermute | solution.py:15
  558.3 29.9 %collective-permute-start.2 = (bf16[256,1024]{0,1:T(8,128)(2,1)}, bf16[256,1024]{0,1:T(8,128)(2,1)S(1)}, u32[]{:S(2)}, u32[]{:S(2)}) collective-permute-start(bf16[256,1024]{0,1:T(8,128)(2,1)} %convert_element_type.269), channel_id=1, source_target_pairs={{0,4},{4,8},{8,12},{12,16},{16,20},{20,24},{24,28},{28,0},{1,5},{5... | collective-permute-start | bytes 1572872 | tf_op jit(solution)/shard_map/while/body/eval_jaxpr/ppermute | solution.py:20
  562.0 31.8 %collective-permute-start.3 = (bf16[256,1024]{0,1:T(8,128)(2,1)}, bf16[256,1024]{0,1:T(8,128)(2,1)S(1)}, u32[]{:S(2)}, u32[]{:S(2)}) collective-permute-start(bf16[256,1024]{0,1:T(8,128)(2,1)} %convert_element_type.271), channel_id=1, source_target_pairs={{0,4},{4,8},{8,12},{12,16},{16,20},{20,24},{24,28},{28,0},{1,5},{5... | collective-permute-start | bytes 1572872 | tf_op jit(solution)/shard_map/while/body/eval_jaxpr/ppermute | solution.py:20
  569.5 25.9 %collective-permute-start.4 = (bf16[256,1024]{0,1:T(8,128)(2,1)S(1)}, bf16[256,1024]{0,1:T(8,128)(2,1)S(1)}, u32[]{:S(2)}, u32[]{:S(2)}) collective-permute-start(bf16[256,1024]{0,1:T(8,128)(2,1)S(1)} %copy.166), channel_id=1, source_target_pairs={{0,4},{4,8},{8,12},{12,16},{16,20},{20,24},{24,28},{1,5},{5,9},{9,... | collective-permute-start | bytes 1572872 | tf_op jit(solution)/shard_map/while/body/eval_jaxpr/ppermute | solution.py:15
  579.6 22.3 %collective-permute-start.5 = (bf16[256,1024]{1,0:T(8,128)(2,1)}, bf16[256,1024]{1,0:T(8,128)(2,1)S(1)}, u32[]{:S(2)}, u32[]{:S(2)}) collective-permute-start(bf16[256,1024]{1,0:T(8,128)(2,1)} %copy.167), channel_id=1, source_target_pairs={{0,4},{4,8},{8,12},{12,16},{16,20},{20,24},{24,28},{1,5},{5,9},{9,... | collective-permute-start | bytes 1572872 | tf_op jit(solution)/shard_map/while/body/eval_jaxpr/ppermute | solution.py:15
  604.7 31.4 %collective-permute-start.2 = (bf16[256,1024]{0,1:T(8,128)(2,1)}, bf16[256,1024]{0,1:T(8,128)(2,1)S(1)}, u32[]{:S(2)}, u32[]{:S(2)}) collective-permute-start(bf16[256,1024]{0,1:T(8,128)(2,1)} %convert_element_type.269), channel_id=1, source_target_pairs={{0,4},{4,8},{8,12},{12,16},{16,20},{20,24},{24,28},{28,0},{1,5},{5... | collective-permute-start | bytes 1572872 | tf_op jit(solution)/shard_map/while/body/eval_jaxpr/ppermute | solution.py:20
  612.0 29.7 %collective-permute-start.3 = (bf16[256,1024]{0,1:T(8,128)(2,1)}, bf16[256,1024]{0,1:T(8,128)(2,1)S(1)}, u32[]{:S(2)}, u32[]{:S(2)}) collective-permute-start(bf16[256,1024]{0,1:T(8,128)(2,1)} %convert_element_type.271), channel_id=1, source_target_pairs={{0,4},{4,8},{8,12},{12,16},{16,20},{20,24},{24,28},{28,0},{1,5},{5... | collective-permute-start | bytes 1572872 | tf_op jit(solution)/shard_map/while/body/eval_jaxpr/ppermute | solution.py:20
  616.6 26.4 %collective-permute-start.4 = (bf16[256,1024]{0,1:T(8,128)(2,1)S(1)}, bf16[256,1024]{0,1:T(8,128)(2,1)S(1)}, u32[]{:S(2)}, u32[]{:S(2)}) collective-permute-start(bf16[256,1024]{0,1:T(8,128)(2,1)S(1)} %copy.166), channel_id=1, source_target_pairs={{0,4},{4,8},{8,12},{12,16},{16,20},{20,24},{24,28},{1,5},{5,9},{9,... | collective-permute-start | bytes 1572872 | tf_op jit(solution)/shard_map/while/body/eval_jaxpr/ppermute | solution.py:15
  625.4 25.5 %collective-permute-start.5 = (bf16[256,1024]{1,0:T(8,128)(2,1)}, bf16[256,1024]{1,0:T(8,128)(2,1)S(1)}, u32[]{:S(2)}, u32[]{:S(2)}) collective-permute-start(bf16[256,1024]{1,0:T(8,128)(2,1)} %copy.167), channel_id=1, source_target_pairs={{0,4},{4,8},{8,12},{12,16},{16,20},{20,24},{24,28},{1,5},{5,9},{9,... | collective-permute-start | bytes 1572872 | tf_op jit(solution)/shard_map/while/body/eval_jaxpr/ppermute | solution.py:15
  653.7 29.4 %collective-permute-start.2 = (bf16[256,1024]{0,1:T(8,128)(2,1)}, bf16[256,1024]{0,1:T(8,128)(2,1)S(1)}, u32[]{:S(2)}, u32[]{:S(2)}) collective-permute-start(bf16[256,1024]{0,1:T(8,128)(2,1)} %convert_element_type.269), channel_id=1, source_target_pairs={{0,4},{4,8},{8,12},{12,16},{16,20},{20,24},{24,28},{28,0},{1,5},{5... | collective-permute-start | bytes 1572872 | tf_op jit(solution)/shard_map/while/body/eval_jaxpr/ppermute | solution.py:20
  659.2 29.6 %collective-permute-start.3 = (bf16[256,1024]{0,1:T(8,128)(2,1)}, bf16[256,1024]{0,1:T(8,128)(2,1)S(1)}, u32[]{:S(2)}, u32[]{:S(2)}) collective-permute-start(bf16[256,1024]{0,1:T(8,128)(2,1)} %convert_element_type.271), channel_id=1, source_target_pairs={{0,4},{4,8},{8,12},{12,16},{16,20},{20,24},{24,28},{28,0},{1,5},{5... | collective-permute-start | bytes 1572872 | tf_op jit(solution)/shard_map/while/body/eval_jaxpr/ppermute | solution.py:20
  663.2 26.6 %collective-permute-start.4 = (bf16[256,1024]{0,1:T(8,128)(2,1)S(1)}, bf16[256,1024]{0,1:T(8,128)(2,1)S(1)}, u32[]{:S(2)}, u32[]{:S(2)}) collective-permute-start(bf16[256,1024]{0,1:T(8,128)(2,1)S(1)} %copy.166), channel_id=1, source_target_pairs={{0,4},{4,8},{8,12},{12,16},{16,20},{20,24},{24,28},{1,5},{5,9},{9,... | collective-permute-start | bytes 1572872 | tf_op jit(solution)/shard_map/while/body/eval_jaxpr/ppermute | solution.py:15
  670.5 23.2 %collective-permute-start.5 = (bf16[256,1024]{1,0:T(8,128)(2,1)}, bf16[256,1024]{1,0:T(8,128)(2,1)S(1)}, u32[]{:S(2)}, u32[]{:S(2)}) collective-permute-start(bf16[256,1024]{1,0:T(8,128)(2,1)} %copy.167), channel_id=1, source_target_pairs={{0,4},{4,8},{8,12},{12,16},{16,20},{20,24},{24,28},{1,5},{5,9},{9,... | collective-permute-start | bytes 1572872 | tf_op jit(solution)/shard_map/while/body/eval_jaxpr/ppermute | solution.py:15
  702.1 146.5 %reduce-scatter.23.cloned.1.call-start = ((), (), s32[]{:S(2)}) async-start(), calls=%async_computation.16 | async-start | bytes 10485760 | tf_op jit(solution)/shard_map/reduce_scatter | solution.py:245
  711.5 211.5 %reduce-scatter.19.cloned.1.call-start = ((), (), s32[]{:S(2)}) async-start(), calls=%async_computation.14 | async-start | bytes 10485760 | tf_op jit(solution)/shard_map/reduce_scatter | solution.py:242
  720.1 270.0 %reduce-scatter.27.cloned.1.call-start = ((), (), s32[]{:S(2)}) async-start(), calls=%async_computation.18 | async-start | bytes 589824
  722.2 335.5 %reduce-scatter.25.cloned.1.call-start = ((), (), s32[]{:S(2)}) async-start(), calls=%async_computation.17 | async-start | bytes 1769472
  777.0 350.9 %reduce-scatter.29.cloned.1.call-start = ((), (), s32[]{:S(2)}) async-start(), calls=%async_computation.19 | async-start | bytes 2359296
  852.5 346.1 %reduce-scatter.21.cloned.1.call-start = ((), (), s32[]{:S(2)}) async-start(), calls=%async_computation.15 | async-start | bytes 2359296 | tf_op jit(solution)/shard_map/reduce_scatter | solution.py:256
  (64 other events, 440.4 us)
Sparse Core Ops, SparseCore 0:
  9.6 46.4 all-gather.4
  57.6 22.5 all-gather.6
  81.8 58.2 all-gather.8
  141.6 58.2 all-gather.10
  291.1 44.2 reduce-scatter.16
  702.2 71.9 reduce-scatter.14
  776.8 71.7 reduce-scatter.22
  851.3 71.6 reduce-scatter.18
  927.0 63.1 reduce-scatter.26
  993.8 63.8 reduce-scatter.24
  1061.3 66.5 reduce-scatter.28
  1131.3 67.3 reduce-scatter.20
where the time goes:
time: 1220 us; the launch traced here: 1210 us
  waiting for transfers between devices  694 us (57%)
  starting transfers between devices  279 us (23%)
  matrix products  72.5 us (6%)
  local copies, waits for them, and re-layouts  54 us (4%)
  other arithmetic  49.1 us (4%)
  blocking collectives  42.3 us (3%)
  between operations  15 us (1%)
    ppermute x30, starting transfers between devices, passed_along(): return lax.ppermute(block, axis, route)  181 us
    ppermute x30, waiting for transfers between devices, passed_along(): return lax.ppermute(block, axis, route)  160 us
    unnamed x15, waiting for transfers between devices  145 us
    ppermute x16, starting transfers between devices, shifted(): lax.ppermute(value, axis, [(i, (i + by) % size) for i in range(size)])  97.7 us
    ppermute x16, waiting for transfers between devices, shifted(): lax.ppermute(value, axis, [(i, (i + by) % size) for i in range(size)])  80.2 us
    reduce_scatter x1, waiting for transfers between devices, per_device(): lax.psum_scatter(grad_down.astype(jnp.bfloat16), 'seg', scatter_dimension...  71.5 us
    reduce_scatter x1, waiting for transfers between devices, per_device(): lax.psum_scatter(grad_up.astype(jnp.bfloat16), 'seg', scatter_dimension=0...  70.5 us
    reduce_scatter x1, waiting for transfers between devices, per_device(): lax.psum_scatter(part_up.astype(jnp.bfloat16), 'seq', scatter_dimension=1...  68.8 us
  transfers between devices with their start and end apart: 58, of which 52 were waited for; matrix products, arithmetic and copies ran while one was open for 11% of the time, Pallas kernels for 0%

commit v1 on v0

--- a/solution.py
+++ b/solution.py
@@ -3,6 +3,8 @@
 import jax
 import jax.numpy as jnp
 from jax import lax
+from jax.experimental import pallas as pl
+from jax.experimental.pallas import tpu as pltpu
 from jax.sharding import PartitionSpec as P
 
 HEADS = 8
@@ -277,9 +279,806 @@
     )
 
 
+MESH = pl.DeviceIdType.MESH
+BF = jnp.bfloat16
+F32 = jnp.float32
+NEAR_FIRST = ((0, 1, 2, 3), (1, 0, 2, 3), (2, 1, 3, 0), (3, 2, 1, 0))
+FAR_FIRST = ((3, 2, 1, 0), (3, 0, 2, 1), (0, 3, 1, 2), (0, 1, 2, 3))
+
+
+def pick(table, row, column):
+    out = jnp.int32(0)
+    for r, line in enumerate(table):
+        for c, entry in enumerate(line):
+            if entry:
+                out = jnp.where((row == r) & (column == c), entry, out)
+    return out
+
+
+def dot_nn(a, b):
+    return lax.dot_general(a, b, (((1,), (0,)), ((), ())), preferred_element_type=F32)
+
+
+def dot_nt(a, b):
+    return lax.dot_general(a, b, (((1,), (1,)), ((), ())), preferred_element_type=F32)
+
+
+def dot_tn(a, b):
+    return lax.dot_general(a, b, (((0,), (0,)), ((), ())), preferred_element_type=F32)
+
+
+def remote(src, dst, send, recv, **place):
+    return pltpu.make_async_remote_copy(
+        src_ref=src, dst_ref=dst, send_sem=send, recv_sem=recv, device_id=place, device_id_type=MESH
+    )
+
+
+def norm_parts(values):
+    center = values - jnp.mean(values, axis=-1, keepdims=True)
+    spread = jnp.mean(center * center, axis=-1, keepdims=True)
+    inverse = lax.rsqrt(spread + 1e-05)
+    return center * inverse, inverse
+
+
+def greet(q, s):
+    barrier = pltpu.get_barrier_semaphore()
+    for d in range(1, 8):
+        pl.semaphore_signal(barrier, 1, device_id={"seq": lax.rem(q + d, 8)}, device_id_type=MESH)
+    for d in range(1, 4):
+        pl.semaphore_signal(barrier, 1, device_id={"seg": lax.rem(s + d, 4)}, device_id_type=MESH)
+    pl.semaphore_wait(barrier, 10)
+
+
+def first_columns(lengths_ref, base, rows):
+    place = base + lax.broadcasted_iota(jnp.int32, (rows, 1), 0)
+    start = jnp.zeros((rows, 1), jnp.int32)
+    bound = jnp.int32(0)
+    for i in range(lengths_ref.shape[1]):
+        bound = bound + lengths_ref[0, i]
+        start = jnp.where(place >= bound, bound, start)
+    return start
+
+
+def seen_mask(start, base_q, base_k, rows, columns):
+    place = base_q + lax.broadcasted_iota(jnp.int32, (rows, columns), 0)
+    key = base_k + lax.broadcasted_iota(jnp.int32, (rows, columns), 1)
+    return (key <= place) & (key >= start)
+
+
+def attend_kernel(
+    x_ref, len_ref, gain_ref, bias_ref, wq_ref, wo_ref, wu_ref, wd_ref,
+    o_ref, wof, wuf, wdf, xs, h1, wh, qkv, of, lse,
+    ob, wd_v, wu_v, wo_v, local_sem, qs, qr, ws, wr, xs_send, xs_recv, os_send, os_recv,
+):
+    q, s = lax.axis_index("seq"), lax.axis_index("seg")
+    z, x = q // 2, q % 2
+    y, c = s // 2, s % 2
+    sib = s + 1 - 2 * c
+    across = (1 - y) * 2 + c
+    corner = (1 - y) * 2 + 1 - c
+    xq = z * 2 + 1 - x
+    T = 256
+    scale = 1.0 / math.sqrt(HEAD_DIM)
+
+    def rows(k, n):
+        return pl.ds(pl.multiple_of(k * n, n), n)
+
+    for j in range(3):
+        wh[rows(s, T), j * 128 : (j + 1) * 128] = wq_ref[:, pl.ds(pl.multiple_of(j * 1024 + q * 128, 128), 128)]
+    greet(q, s)
+
+    def wq_copy(k, quarter, place):
+        return remote(wh.at[rows(quarter, T)], wh.at[rows(quarter, T)], qs.at[k], qr.at[k], seg=place)
+
+    q_across, q_sib = wq_copy(0, s, across), wq_copy(1, s, sib)
+    q_across.start()
+    q_sib.start()
+
+    def x_copy(b, k, to):
+        src = xs.at[rows(b, T)]
+        return remote(src, src, xs_send.at[k], xs_recv.at[b], seq=to)
+
+    xs[rows(q, T)] = x_ref[...]
+
+    half = wd_ref.shape[0] // 2
+
+    def part(full, quarter, size, start=0, n=None):
+        n = size if n is None else n
+        return full.at[pl.ds(pl.multiple_of(quarter * size + start, 16), n)]
+
+    down_half = x * half
+    y_down = remote(wd_ref.at[pl.ds(pl.multiple_of(down_half, half), half)],
+                    part(wdf, s, 2 * half, down_half, half), ws.at[0], wr.at[0], seg=across)
+    y_up = remote(wu_ref, part(wuf, s, T), ws.at[1], wr.at[1], seg=across)
+    y_out = remote(wo_ref, part(wof, s, T), ws.at[2], wr.at[2], seg=across)
+    s_down = remote(wd_ref, part(wdf, s, 2 * half), ws.at[3], wr.at[3], seg=sib)
+    s_up = remote(wu_ref, part(wuf, s, T), ws.at[4], wr.at[4], seg=sib)
+    s_out = remote(wo_ref, part(wof, s, T), ws.at[5], wr.at[5], seg=sib)
+    got = part(wdf, across, 2 * half, down_half, half)
+    x_down = remote(got, got, ws.at[6], wr.at[6], seq=xq)
+    f_down_a = remote(got, got, ws.at[7], wr.at[7], seg=sib)
+    other = part(wdf, across, 2 * half, half - down_half, half)
+    f_down_b = remote(other, other, ws.at[8], wr.at[8], seg=sib)
+    up = part(wuf, across, T)
+    f_up = remote(up, up, ws.at[9], wr.at[9], seg=sib)
+    out = part(wof, across, T)
+    f_out = remote(out, out, ws.at[10], wr.at[10], seg=sib)
+    own_in = (
+        pltpu.make_async_copy(wd_ref, wd_v, local_sem.at[0]),
+        pltpu.make_async_copy(wu_ref, wu_v, local_sem.at[1]),
+        pltpu.make_async_copy(wo_ref, wo_v, local_sem.at[2]),
+    )
+    own = (
+        pltpu.make_async_copy(wd_v, part(wdf, s, 2 * half), local_sem.at[4]),
+        pltpu.make_async_copy(wu_v, part(wuf, s, T), local_sem.at[5]),
+        pltpu.make_async_copy(wo_v, part(wof, s, T), local_sem.at[6]),
+    )
+    for copy in (y_down, y_up, y_out):
+        copy.start()
+
+    q_across.wait_recv()
+    q_pass = wq_copy(2, across, sib)
+    q_pass.start()
+    for copy in (s_down, s_up, s_out) + own_in:
+        copy.start()
+    q_sib.wait_recv()
+    q_pass.wait_recv()
+
+    gain, bias = gain_ref[...], bias_ref[...]
+
+    def project(b):
+        unit, _ = norm_parts(xs[rows(b, T)].astype(F32))
+        low = (unit * gain + bias).astype(BF)
+        h1[rows(b, T)] = low
+        qkv[rows(b, T)] = dot_nn(low, wh[...]).astype(BF)
+
+    def z_step(i, _):
+        zz = pick(NEAR_FIRST, z, i)
+        b = zz * 2 + x
+
+        @pl.when(i > 0)
+        def _():
+            x_copy(b, 0, q).wait_recv()
+
+        @pl.when((zz <= z) & (z < 3))
+        def _():
+            x_copy(b, zz, q + 2).start()
+
+        @pl.when((zz >= z) & (z > 0))
+        def _():
+            x_copy(b, 4 + zz, q - 2).start()
+
+        x_copy(b, 8 + zz, xq).start()
+        project(b)
+        return 0
+
+    lax.fori_loop(0, 4, z_step, 0)
+    for arrived, copy in zip(own_in, own):
+        arrived.wait()
+        copy.start()
+    y_down.wait_recv()
+    x_down.start()
+    f_down_a.start()
+
+    def x_step(i, _):
+        b = pick(NEAR_FIRST, z, i) * 2 + 1 - x
+        x_copy(b, 0, q).wait_recv()
+        project(b)
+        return 0
+
+    lax.fori_loop(0, 4, x_step, 0)
+
+    def z_end(zz, _):
+        @pl.when((zz <= z) & (z < 3))
+        def _():
+            x_copy(zz * 2 + x, zz, q + 2).wait_send()
+
+        @pl.when((zz >= z) & (z > 0))
+        def _():
+            x_copy(zz * 2 + x, 4 + zz, q - 2).wait_send()
+
+        x_copy(zz * 2 + x, 8 + zz, xq).wait_send()
+        return 0
+
+    def o_copy(i, sender):
+        columns = pl.ds(pl.multiple_of(sender * 128, 128), 128)
+        return remote(ob.at[i], o_ref.at[:, columns], os_send.at[i], os_recv.at[sender], seq=i)
+
+    mine = pltpu.make_async_copy(
+        ob.at[q], o_ref.at[:, pl.ds(pl.multiple_of(q * 128, 128), 128)], local_sem.at[3]
+    )
+    for i in range(8):
+        n = (i + 1) * T
+        start = first_columns(len_ref, i * T, T)
+        scores = dot_nt(qkv[i * T : n, :128], qkv[:n, 128:256]) * scale
+        scores = jnp.where(seen_mask(start, i * T, 0, T, n), scores, -1e30)
+        top = jnp.max(scores, axis=1, keepdims=True)
+        weights = jnp.exp(scores - top)
+        total = jnp.sum(weights, axis=1, keepdims=True)
+        mixed = dot_nn(weights.astype(BF), qkv[:n, 256:384]) / total
+        of[i * T : n] = mixed
+        lse[i * T : n] = top + jnp.log(total)
+        ob[i] = mixed.astype(BF)
+
+        @pl.when(q != i)
+        def _():
+            o_copy(i, q).start()
+
+        @pl.when(q == i)
+        def _():
+            mine.start()
+
+    y_up.wait_recv()
+    f_up.start()
+    y_out.wait_recv()
+    f_out.start()
+    x_down.wait_recv()
+    f_down_b.start()
+
+    lax.fori_loop(0, 4, z_end, 0)
+    for i in range(8):
+        @pl.when(q != i)
+        def _():
+            o_copy(i, q).wait_send()
+            o_copy(i, i).wait_recv()
+
+    mine.wait()
+    for copy in own:
+        copy.wait()
+    for copy in (q_across, q_sib, q_pass):
+        copy.wait_send()
+    for copy in (y_down, y_up, y_out, s_down, s_up, s_out, x_down, f_down_a, f_down_b, f_up, f_out):
+        copy.wait_send()
+    for copy in (s_down, s_up, s_out, f_down_a, f_down_b, f_up, f_out):
+        copy.wait_recv()
+
+
+VM = pl.BlockSpec(memory_space=pltpu.VMEM)
+HB = pl.BlockSpec(memory_space=pl.ANY)
+SM = pl.BlockSpec(memory_space=pltpu.SMEM)
+
+
+def attend(x, lengths, gain, bias, wq, wo, wu, wd):
+    S = jax.ShapeDtypeStruct
+    dma = pltpu.SemaphoreType.DMA
+    return pl.pallas_call(
+        attend_kernel,
+        out_shape=(
+            S((256, 1024), BF), S((1024, 1024), BF), S((1024, 4096), BF), S((4096, 1024), BF),
+            S((2048, 1024), BF), S((2048, 1024), BF), S((1024, 384), BF), S((2048, 384), BF),
+            S((2048, 128), F32), S((2048, 1), F32),
+        ),
+        in_specs=[VM, SM, VM, VM, VM, HB, HB, HB],
+        out_specs=(VM, HB, HB, HB, VM, VM, VM, VM, VM, VM),
+        scratch_shapes=[
+            pltpu.VMEM((8, 256, 128), BF), pltpu.VMEM((1024, 1024), BF), pltpu.VMEM((256, 4096), BF),
+            pltpu.VMEM((256, 1024), BF), dma((7,)), dma((3,)), dma((3,)), dma((11,)), dma((11,)),
+            dma((12,)), dma((8,)), dma((8,)), dma((8,)),
+        ],
+        compiler_params=pltpu.CompilerParams(
+            collective_id=0, has_side_effects=True, vmem_limit_bytes=58 * 2**20
+        ),
+        cost_estimate=pl.CostEstimate(flops=5 * 10**9, bytes_accessed=40 * 2**20, transcendentals=2 * 2**20),
+        name="attend",
+    )(x, lengths, gain, bias, wq, wo, wu, wd)
+
+
+def gelu_parts(u):
+    root = math.sqrt(2.0 / math.pi)
+    square = u * u
+    t = jnp.tanh(root * (u + 0.044715 * (square * u)))
+    value = 0.5 * u * (1.0 + t)
+    slope = 0.5 * (1.0 + t) + 0.5 * u * (1.0 - t * t) * (root * (1.0 + 0.134145 * square))
+    return value, slope
+
+
+def norm_back(grad, gain, unit, inverse):
+    through = grad * gain
+    a = jnp.mean(through, axis=-1, keepdims=True)
+    b = jnp.mean(through * unit, axis=-1, keepdims=True)
+    return inverse * (through - a - unit * b)
+
+
+def ffn_kernel(
+    x_ref, o_ref, g_ref, gain_ref, bias_ref, wo_ref, wu_ref, wd_ref,
+    result_ref, dx_ref, do_ref, sums_ref, pack_ref,
+    pack, middle, unit_v, inv_v, h2, acc, dh2, up_sem, down_sem, out_sem,
+):
+    f = pl.program_id(0)
+    T = 256
+
+    @pl.when(f == 0)
+    def _():
+        value = x_ref[...].astype(F32) + dot_nn(o_ref[...], wo_ref[...])
+        middle[...] = value
+        unit, inverse = norm_parts(value)
+        unit_v[...] = unit
+        inv_v[...] = inverse
+        h2[...] = (unit * gain_ref[...] + bias_ref[...]).astype(BF)
+        acc[...] = jnp.zeros_like(acc)
+        dh2[...] = jnp.zeros_like(dh2)
+
+    g = g_ref[...]
+    value, slope = gelu_parts(dot_nn(h2[...], wu_ref[...]))
+    low = value.astype(BF)
+    acc[...] += dot_nn(low, wd_ref[...])
+    du = (slope * dot_nt(g, wd_ref[...])).astype(BF)
+    dh2[...] += dot_nt(du, wu_ref[...])
+    pack[:, f, :, 0:512] = dot_tn(h2[...], du).astype(BF).reshape(4, T, 512)
+    down = dot_tn(low, g).astype(BF)
+    base = 512 + (f % 2) * 256
+    for jj in range(2):
+        for k in range(8):
+            pack[f // 2, k, :, pl.ds(pl.multiple_of(base + jj * 128, 128), 128)] = down[
+                jj * T : (jj + 1) * T, k * 128 : (k + 1) * 128
+            ]
+
+    def up_copy(n):
+        return pltpu.make_async_copy(
+            pack.at[:, n, :, 0:512], pack_ref.at[:, n, :, 0:512], up_sem.at[n]
+        )
+
+    def down_copy(n):
+        columns = pl.ds(pl.multiple_of(512 + (n % 2) * 256, 256), 256)
+        return pltpu.make_async_copy(
+            pack.at[n // 2, :, :, columns], pack_ref.at[n // 2, :, :, columns], down_sem.at[n]
+        )
+
+    up_copy(f).start()
+    down_copy(f).start()
+
+    @pl.when(f == 7)
+    def _():
+        result_ref[...] = (middle[...] + acc[...]).astype(BF)
+        unit, grad = unit_v[...], dh2[...]
+        sums_ref[0:1] = jnp.sum(grad * unit, axis=0, keepdims=True)
+        sums_ref[1:2] = jnp.sum(grad, axis=0, keepdims=True)
+        dx = g.astype(F32) + norm_back(grad, gain_ref[...], unit, inv_v[...])
+        dx_ref[...] = dx
+        dy = dx.astype(BF)
+        do_ref[...] = dot_nt(dy, wo_ref[...]).astype(BF)
+        out = dot_tn(o_ref[...], dy).astype(BF)
+        for quarter in range(4):
+            for k in range(8):
+                pack[quarter, k, :, 1024:1152] = out[
+                    quarter * T : (quarter + 1) * T, k * 128 : (k + 1) * 128
+                ]
+        copy = pltpu.make_async_copy(pack.at[:, :, :, 1024:1152], pack_ref.at[:, :, :, 1024:1152], out_sem)
+        copy.start()
+        for n in range(8):
+            up_copy(n).wait()
+            down_copy(n).wait()
+        copy.wait()
+
+
+def ffn(x, o, g, gain, bias, wo, wu, wd):
+    S = jax.ShapeDtypeStruct
+    dma = pltpu.SemaphoreType.DMA
+    whole = lambda r, n: pl.BlockSpec((r, n), lambda f: (0, 0))
+    return pl.pallas_call(
+        ffn_kernel,
+        grid=(8,),
+        out_shape=(
+            S((256, 1024), BF), S((256, 1024), F32), S((256, 1024), BF), S((2, 1024), F32),
+            S((4, 8, 256, 1152), BF),
+        ),
+        in_specs=[
+            whole(256, 1024), whole(256, 1024), whole(256, 1024), whole(1, 1024), whole(1, 1024),
+            whole(1024, 1024), pl.BlockSpec((1024, 512), lambda f: (0, f)),
+            pl.BlockSpec((512, 1024), lambda f: (f, 0)),
+        ],
+        out_specs=(
+            whole(256, 1024), whole(256, 1024), whole(256, 1024), whole(2, 1024), HB,
+        ),
+        scratch_shapes=[
+            pltpu.VMEM((4, 8, 256, 1152), BF), pltpu.VMEM((256, 1024), F32), pltpu.VMEM((256, 1024), F32),
+            pltpu.VMEM((256, 1), F32), pltpu.VMEM((256, 1024), BF), pltpu.VMEM((256, 1024), F32),
+            pltpu.VMEM((256, 1024), F32), dma((8,)), dma((8,)), dma,
+        ],
+        compiler_params=pltpu.CompilerParams(
+            dimension_semantics=("arbitrary",), vmem_limit_bytes=58 * 2**20
+        ),
+        cost_estimate=pl.CostEstimate(flops=15 * 10**9, bytes_accessed=40 * 2**20, transcendentals=2**20),
+        name="ffn",
+    )(x, o, g, gain, bias, wo, wu, wd)
+
+
+def grads_kernel(
+    pack_ref, do_ref, dx_ref, sums2_ref, xs_ref, h1_ref, wh_ref, qkv_ref, of_ref, lse_ref, len_ref, gain_ref,
+    dx_out, gqkv_out, gout_out, gup_out, gdown_out, sums_out,
+    load, core_r, y_r, x_r, z_r, doh, dq, dk, dv, dh_s, dhx_r, dhz_r, gq, gq_b, gq_c, gq_y, gq_s, gq_r,
+    vec, vec_r, xbuf, hbuf,
+    load_sem, cs, cr, ys, yr, gxs, gxr, gzs, gzr, dos, dor, dxs, dxr, dzs, dzr, qs, qr, vs, vr, blk_sem,
+):
+    q, s = lax.axis_index("seq"), lax.axis_index("seg")
+    z, x = q // 2, q % 2
+    y, c = s // 2, s % 2
+    sib = s + 1 - 2 * c
+    across = (1 - y) * 2 + c
+    xq = z * 2 + 1 - x
+    T = 256
+    scale = 1.0 / math.sqrt(HEAD_DIM)
+
+    def rows(k, n):
+        return pl.ds(pl.multiple_of(k * n, n), n)
+
+    def lanes(k):
+        return pl.ds(pl.multiple_of(k * 128, 128), 128)
+
+    def dest(k):
+        return pick(FAR_FIRST, z, k // 2) * 2 + jnp.where(k % 2 == 0, 1 - x, x)
+
+    greet(q, s)
+
+    def do_copy(b, sender):
+        return remote(do_ref.at[:, lanes(b)], doh.at[rows(sender, T)], dos.at[b], dor.at[sender], seq=b)
+
+    do_mine = pltpu.make_async_copy(do_ref.at[:, lanes(q)], doh.at[rows(q, T)], blk_sem.at[4])
+    do_mine.start()
+    for b in range(8):
+        @pl.when(q != b)
+        def _():
+            do_copy(b, q).start()
+
+    def core_copy(t):
+        return remote(pack_ref.at[:, 1 - c, t], core_r.at[t], cs.at[t], cr.at[t], seg=sib)
+
+    def load_copy(k):
+        return pltpu.make_async_copy(pack_ref.at[:, c, dest(k)], load.at[k % 2], load_sem.at[k % 2])
+
+    def y_copy(t):
+        return remote(core_r.at[t, 1 - y], y_r.at[t], ys.at[t], yr.at[t], seg=across)
+
+    def start_core(k, _):
+        core_copy(dest(k)).start()
+        return 0
+
+    lax.fori_loop(0, 8, start_core, 0)
+    load_copy(0).start()
+
+    def core_step(k, _):
+        t = dest(k)
+
+        @pl.when(k < 7)
+        def _():
+            load_copy(k + 1).start()
+
+        load_copy(k).wait()
+        core_copy(t).wait_recv()
+        for part in range(2):
+            core_r[t, part] = (core_r[t, part].astype(F32) + load[k % 2, part].astype(F32)).astype(BF)
+
+        @pl.when(k < 5)
+        def _():
+            y_copy(t).start()
+
+        return 0
+
+    lax.fori_loop(0, 8, core_step, 0)
+    for b in range(8):
+        @pl.when(q != b)
+        def _():
+            do_copy(b, b).wait_recv()
+
+    do_mine.wait()
+
+    dk[...] = jnp.zeros_like(dk)
+    dv[...] = jnp.zeros_like(dv)
+    for i in range(8):
+        top = i * T
+        start = first_columns(len_ref, top, T)
+        query = qkv_ref[top : top + T, :128]
+        grad = doh[top : top + T]
+        delta = jnp.sum(grad.astype(F32) * of_ref[top : top + T], axis=1, keepdims=True)
+        log_total = lse_ref[top : top + T]
+        total = jnp.zeros((T, 128), F32)
+        for base in range(0, top + T, 1024):
+            n = min(1024, top + T - base)
+            keys = qkv_ref[base : base + n, 128:256]
+            probs = jnp.exp(dot_nt(query, keys) * scale - log_total)
+            probs = jnp.where(seen_mask(start, top, base, T, n), probs, 0.0)
+            dp = dot_nt(grad, qkv_ref[base : base + n, 256:384])
+            ds = (probs * (dp - delta)).astype(BF)
+            dv[base : base + n] += dot_tn(probs.astype(BF), grad)
+            dk[base : base + n] += dot_tn(ds, query)
+            total += dot_nn(ds, keys)
+        dq[top : top + T] = total
+
+    gq[...] = jnp.zeros_like(gq)
+    vec[...] = jnp.zeros_like(vec)
+    vec[2:4] = sums2_ref[...]
+
+    def block_of(i):
+        return pick(FAR_FIRST, z, i % 4) * 2 + jnp.where(i < 4, 1 - x, x)
+
+    def x_load(i):
+        return pltpu.make_async_copy(xs_ref.at[rows(block_of(i), T)], xbuf.at[i % 2], blk_sem.at[i % 2])
+
+    def h_load(i):
+        return pltpu.make_async_copy(h1_ref.at[rows(block_of(i), T)], hbuf.at[i % 2], blk_sem.at[2 + i % 2])
+
+    def dhx_copy(zz):
+        return remote(dh_s.at[zz * 2 + 1 - x], dhx_r.at[zz], dxs.at[zz], dxr.at[zz], seq=xq)
+
+    x_load(0).start()
+    h_load(0).start()
+
+    def block_step(i, _):
+        b = block_of(i)
+
+        @pl.when(i < 7)
+        def _():
+            x_load(i + 1).start()
+            h_load(i + 1).start()
+
+        at = rows(b, T)
+        low = jnp.concatenate([dq[at] * scale, dk[at] * scale, dv[at]], axis=1).astype(BF)
+        dh = dot_nt(low, wh_ref[...])
+        dh_s[b] = dh.astype(BF)
+
+        @pl.when(i < 4)
+        def _():
+            dhx_copy(pick(FAR_FIRST, z, i % 4)).start()
+
+        x_load(i).wait()
+        h_load(i).wait()
+        gq[...] += dot_tn(hbuf[i % 2], low)
+        unit, _ = norm_parts(xbuf[i % 2].astype(F32))
+        vec[0:1] += jnp.sum(dh * unit, axis=0, keepdims=True)
+        vec[1:2] += jnp.sum(dh, axis=0, keepdims=True)
+        return 0
+
+    lax.fori_loop(0, 8, block_step, 0)
+
+    gq_b[...] = gq[...].astype(BF).reshape(2, 2, T, 384)
+    q_core = remote(gq_b.at[:, 1 - c], gq_c, qs.at[0], qr.at[0], seg=sib)
+    q_core.start()
+    v_core = remote(vec, vec_r.at[0], vs.at[0], vr.at[0], seg=sib)
+    v_core.start()
+    q_core.wait_recv()
+    for part in range(2):
+        gq_c[part] = (gq_c[part].astype(F32) + gq_b[part, c].astype(F32)).astype(BF)
+    q_y = remote(gq_c.at[1 - y], gq_y, qs.at[1], qr.at[1], seg=across)
+    q_y.start()
+    v_core.wait()
+    vec[...] += vec_r[0]
+    v_y = remote(vec, vec_r.at[1], vs.at[1], vr.at[1], seg=across)
+    v_y.start()
+
+    def start_y(k, _):
+        y_copy(dest(k)).start()
+        return 0
+
+    lax.fori_loop(5, 8, start_y, 0)
+
+    def gx_copy(zz):
+        return remote(core_r.at[zz * 2 + 1 - x, y], x_r.at[zz], gxs.at[zz], gxr.at[zz], seq=xq)
+
+    def line_slot(d, place):
+        return jnp.where(d == place, 4, d)
+
+    def line(src, into, send, recv, d):
+        up = remote(src, into.at[d], send.at[d], recv.at[d], seq=q + 2)
+        low = line_slot(d, z - 1)
+        down = remote(src, into.at[low], send.at[d], recv.at[low], seq=q - 2)
+        return up, down
+
+    def come(into, recv, slot):
+        return remote(into.at[slot], into.at[slot], recv.at[slot], recv.at[slot], seq=xq)
+
+    def pass_on(value, keep, into, send, recv, d):
+        has_in = jnp.where(d > z, z > 0, z < 3)
+
+        @pl.when(d != z)
+        def _():
+            @pl.when(has_in)
+            def _():
+                come(into, recv, d).wait_recv()
+                keep[...] = (value() + into[d].astype(F32)).astype(BF)
+
+            @pl.when(jnp.logical_not(has_in))
+            def _():
+                keep[...] = value().astype(BF)
+
+            up, down = line(keep, into, send, recv, d)
+
+            @pl.when(d > z)
+            def _():
+                up.start()
+
+            @pl.when(d < z)
+            def _():
+                down.start()
+
+    def line_step(j, _):
+        d = pick(FAR_FIRST, z, j)
+        own, other = d * 2 + x, d * 2 + 1 - x
+        y_copy(other).wait_recv()
+        core_r[other, y] = (core_r[other, y].astype(F32) + y_r[other].astype(F32)).astype(BF)
+        gx_copy(d).start()
+        dhx_copy(d).wait_recv()
+        pass_on(
+            lambda: dh_s[own].astype(F32) + dhx_r[d].astype(F32), dh_s.at[own], dhz_r, dzs, dzr, d
+        )
+        y_copy(own).wait_recv()
+        gx_copy(d).wait_recv()
+        pass_on(
+            lambda: core_r[own, y].astype(F32) + y_r[own].astype(F32) + x_r[d].astype(F32),
+            core_r.at[own, y], z_r, gzs, gzr, d,
+        )
+        return 0
+
+    lax.fori_loop(0, 2, line_step, 0)
+    v_y.wait()
+    vec[...] += vec_r[1]
+    v_x = remote(vec, vec_r.at[2], vs.at[2], vr.at[2], seq=xq)
+    v_x.start()
+    q_y.wait_recv()
+    gq_s[...] = (gq_c[y].astype(F32) + gq_y[...].astype(F32)).astype(BF)
+
+    def column_copy(j):
+        column = j * 1024 + q * 128
+        owner, slot = column // 384, (column % 384) // 128
+        copy = remote(gq_s.at[:, j * 128 : (j + 1) * 128], gq_r.at[slot], qs.at[2 + j], qr.at[2 + slot], seq=owner)
+        local = pltpu.make_async_copy(gq_s.at[:, j * 128 : (j + 1) * 128], gq_r.at[slot], qr.at[2 + slot])
+        return owner, copy, local
+
+    for j in range(3):
+        owner, copy, local = column_copy(j)
+
+        @pl.when(owner != q)
+        def _():
+            copy.start()
+
+        @pl.when(owner == q)
+        def _():
+            local.start()
+
+    lax.fori_loop(2, 3, line_step, 0)
+    v_x.wait()
+    vec[...] += vec_r[2]
+
+    def v_copy(zz, sender):
+        return remote(vec, vec_r.at[3 + sender], vs.at[3 + zz], vr.at[3 + sender], seq=zz * 2 + x)
+
+    for zz in range(4):
+        @pl.when(zz != z)
+        def _():
+            v_copy(zz, z).start()
+
+    lax.fori_loop(3, 4, line_step, 0)
+
+    def arrived(into, recv):
+        @pl.when(z > 0)
+        def _():
+            come(into, recv, z).wait_recv()
+
+        @pl.when(z == 0)
+        def _():
+            into[0] = jnp.zeros_like(into[0])
+
+        @pl.when(z < 3)
+        def _():
+            come(into, recv, 4).wait_recv()
+
+        @pl.when(z == 3)
+        def _():
+            into[4] = jnp.zeros_like(into[4])
+
+        return into[z].astype(F32) + into[4].astype(F32)
+
+    dh = dh_s[q].astype(F32) + dhx_r[z].astype(F32) + arrived(dhz_r, dzr)
+    mine = pltpu.make_async_copy(xs_ref.at[rows(q, T)], xbuf.at[0], blk_sem.at[0])
+    mine.start()
+    mine.wait()
+    unit, inverse = norm_parts(xbuf[0].astype(F32))
+    dx_out[...] = dx_ref[...] + norm_back(dh, gain_ref[...], unit, inverse)
+    total = core_r[q, y].astype(F32) + y_r[q].astype(F32) + x_r[z].astype(F32) + arrived(z_r, gzr)
+    gup_out[...] = total[:, :512]
+    for j in range(4):
+        gdown_out[j * T : (j + 1) * T] = total[:, 512 + j * 128 : 640 + j * 128]
+    gout_out[...] = total[:, 1024:]
+    for slot in range(3):
+        come(gq_r, qr.at[pl.ds(2, 3)], slot).wait_recv()
+        gqkv_out[:, slot * 128 : (slot + 1) * 128] = gq_r[slot].astype(F32)
+    vec_r[3 + z] = vec[...]
+    for zz in range(4):
+        @pl.when(zz != z)
+        def _():
+            v_copy(zz, zz).wait_recv()
+
+    sums_out[...] = (vec_r[3] + vec_r[4] + vec_r[5] + vec_r[6])[:4]
+
+    for b in range(8):
+        @pl.when(q != b)
+        def _():
+            do_copy(b, q).wait_send()
+
+    def sent(t, _):
+        core_copy(t).wait_send()
+        y_copy(t).wait_send()
+        return 0
+
+    lax.fori_loop(0, 8, sent, 0)
+
+    def sent_lines(d, _):
+        gx_copy(d).wait_send()
+        dhx_copy(d).wait_send()
+
+        @pl.when(d != z)
+        def _():
+            line(dh_s.at[d * 2 + x], dhz_r, dzs, dzr, d)[0].wait_send()
+            line(core_r.at[d * 2 + x, y], z_r, gzs, gzr, d)[0].wait_send()
+
+        return 0
+
+    lax.fori_loop(0, 4, sent_lines, 0)
+    q_core.wait_send()
+    q_y.wait_send()
+    for j in range(3):
+        owner, copy, _ = column_copy(j)
+
+        @pl.when(owner != q)
+        def _():
+            copy.wait_send()
+
+    for zz in range(4):
+        @pl.when(zz != z)
+        def _():
+            v_copy(zz, z).wait_send()
+
+
+def grads(pack, do, dx, sums2, xs, h1, wh, qkv, of, lse, lengths, gain):
+    S = jax.ShapeDtypeStruct
+    V = pltpu.VMEM
+    dma = pltpu.SemaphoreType.DMA
+    return pl.pallas_call(
+        grads_kernel,
+        out_shape=(
+            S((256, 1024), F32), S((256, 384), F32), S((256, 128), F32), S((256, 512), F32),
+            S((1024, 128), F32), S((4, 1024), F32),
+        ),
+        in_specs=[HB, VM, VM, VM, HB, HB, VM, VM, VM, VM, SM, VM],
+        out_specs=(VM,) * 6,
+        scratch_shapes=[
+            V((2, 2, 256, 1152), BF), V((8, 2, 256, 1152), BF), V((8, 256, 1152), BF), V((4, 256, 1152), BF),
+            V((5, 256, 1152), BF), V((2048, 128), BF), V((2048, 128), F32), V((2048, 128), F32),
+            V((2048, 128), F32), V((8, 256, 1024), BF), V((4, 256, 1024), BF), V((5, 256, 1024), BF),
+            V((1024, 384), F32), V((2, 2, 256, 384), BF), V((2, 256, 384), BF), V((256, 384), BF),
+            V((256, 384), BF), V((3, 256, 128), BF), V((8, 1024), F32), V((7, 8, 1024), F32),
+            V((2, 256, 1024), BF), V((2, 256, 1024), BF),
+            dma((2,)), dma((8,)), dma((8,)), dma((8,)), dma((8,)), dma((4,)), dma((4,)), dma((4,)), dma((5,)),
+            dma((8,)), dma((8,)), dma((4,)), dma((4,)), dma((4,)), dma((5,)), dma((5,)), dma((5,)),
+            dma((7,)), dma((7,)), dma((5,)),
+        ],
+        compiler_params=pltpu.CompilerParams(
+            collective_id=1, has_side_effects=True, vmem_limit_bytes=60 * 2**20
+        ),
+        cost_estimate=pl.CostEstimate(flops=8 * 10**9, bytes_accessed=40 * 2**20, transcendentals=2 * 2**20),
+        name="grads",
+    )(pack.reshape(2, 2, 8, 256, 1152), do, dx, sums2, xs, h1, wh, qkv, of, lse, lengths, gain)
+
+
+def per_device_fast(
+    tokens, article_lengths, gain_one, bias_one, w_qkv, w_out, gain_two, bias_two, w_up, w_down, cotangent
+):
+    x = tokens[0]
+    o, wo, wu, wd, xs, h1, wh, qkv, of, lse = attend(
+        x, article_lengths, gain_one[None], bias_one[None], w_qkv, w_out, w_up, w_down
+    )
+    result, dx, do, sums2, pack = ffn(
+        x, o, cotangent[0], gain_two[None], bias_two[None], wo, wu, wd
+    )
+    dx, gqkv, gout, gup, gdown, sums = grads(
+        pack, do, dx, sums2, xs, h1, wh, qkv, of, lse, article_lengths, gain_one[None]
+    )
+    return (result[None], dx[None], sums[0], sums[1], gqkv, gout, sums[2], sums[3], gup, gdown)
+
+
 def solution(mesh):
+    one_pair = mesh.shape["seq"] == HEADS and mesh.shape["seg"] == 4
     return jax.shard_map(
-        per_device,
+        per_device_fast if one_pair else per_device,
         mesh=mesh,
         in_specs=(
             P("seg", "seq", None),

time: 1220 us -> 300 us (0.25)
  waiting for transfers between devices: 694 us -> 0 us
  Pallas kernels: 0 us -> 287 us
  starting transfers between devices: 279 us -> 0 us
  matrix products: 72.5 us -> 0 us
  other arithmetic: 49.1 us -> 0 us
  local copies, waits for them, and re-layouts: 54 us -> 9.78 us
  blocking collectives: 42.3 us -> 0 us
  between operations: 15 us -> 0.68 us
    pallas_call x0 -> x3, Pallas kernels: none -> 287 us  [the longest x1 160 us: grads(): pl.pallas_call(grads_kernel, out_shape=(S((256, 1024), F32), S((256, 384)...]
    ppermute x46 -> x0, starting transfers between devices: 279 us -> none  [the longest x30 181 us: passed_along(): return lax.ppermute(block, axis, route)]
    reduce_scatter x5 -> x0, waiting for transfers between devices: 263 us -> none  [the longest x1 71.5 us: per_device(): lax.psum_scatter(grad_down.astype(jnp.bfloat16), 'seg', scatter_dimension...]
    ppermute x46 -> x0, waiting for transfers between devices: 240 us -> none  [the longest x30 160 us: passed_along(): return lax.ppermute(block, axis, route)]
    unnamed x15 -> x0, waiting for transfers between devices: 145 us -> none
    dot_general x19 -> x0, matrix products: 72.5 us -> none  [the longest x1 11.5 us: per_device(): jnp.einsum('td,fd->tf', grad_top_low, full_down, preferred_element_type=j...]
    all_gather x4 -> x0, waiting for transfers between devices: 45.2 us -> none  [the longest x1 45.1 us: per_device(): lax.all_gather(w_qkv, 'seg', axis=0, tiled=True)]
    psum x1 -> x0, blocking collectives: 42.3 us -> none  [per_device(): lax.psum((grad_gain_one, grad_bias_one, grad_gain_two, grad_bias_two), ('...]
  transfers between devices with their start and end apart: 58 -> 0, of which waited for: 52 -> 0; matrix products, arithmetic and copies ran while one was open for 11% -> 0% of each run, Pallas kernels for 0% -> 0%
where the time goes in v1:
time: 300 us; the launch traced here: 297 us
  Pallas kernels  287 us (96%)
  local copies, waits for them, and re-layouts  9.78 us (3%)
    pallas_call x1, Pallas kernels, grads(): pl.pallas_call(grads_kernel, out_shape=(S((256, 1024), F32), S((256, 384)...  160 us
    pallas_call x1, Pallas kernels, attend(): pl.pallas_call(attend_kernel, out_shape=(S((256, 1024), BF), S((1024, 102...  101 us
    pallas_call x1, Pallas kernels, ffn(): pl.pallas_call(ffn_kernel, grid=(8,), out_shape=(S((256, 1024), BF), S((2...  26.2 us
    unnamed x7, local copies, waits for them, and re-layouts  8.3 us

profile of v1, /device:TPU:4, one launch (start us, length us, event | category | flops | bytes accessed | tf_op | source)
XLA Modules:
  0.0 297.0 jit_solution(15305997836647260367)
XLA Ops:
  0.6 100.8 %attend.1 = (bf16[256,1024]{1,0:T(8,128)(2,1)}, bf16[1024,1024]{1,0:T(8,128)(2,1)}, bf16[1024,4096]{1,0:T(8,128)(2,1)}, bf16[4096,1024]{1,0:T(8,128)(2,1)}, bf16...) custom-call(bf16[256,1024]{1,0:T(8,128)(2,1)} %bitcast.21, ...), custom_call_target="tpu_custom_call" | custom-call | flops 5000000000 | bytes 41943040 | tf_op jit(solution)/shard_map/attend/pallas_call | solution.py:544
  101.4 26.2 %ffn.1 = (bf16[256,1024]{1,0:T(8,128)(2,1)}, f32[256,1024]{1,0:T(8,128)}, bf16[256,1024]{1,0:T(8,128)(2,1)}, f32[2,1024]{1,0:T(2,128)}, bf16[4,8,256,1152]{3,2,1,0:T(8,128)(2,1)}) custom-call(bf16[256,1024]{1,0:T(8,128)(2,1)} %bitcast.22, bf16[256,1024]{1,0:T(8,128)(2,1)} %get-tuple-element.31.o_ref, bf16[256,1024]{1,0:T(8,128)(2,1)} %bitcast.23, ...), custom_call_target="tpu_custom_call" | custom-call | flops 15000000512 | bytes 41943040 | tf_op jit(solution)/shard_map/ffn/pallas_call | solution.py:658
  127.7 159.5 %grads.1 = (f32[256,1024]{1,0:T(8,128)}, f32[256,384]{1,0:T(8,128)}, f32[256,128]{1,0:T(8,128)}, f32[256,512]{1,0:T(8,128)}, f32[1024,128]{1,0:T(8,128)}, /*index=5*/f32[4,1024]{1,0:T(4,128)}) custom-call(bf16[2,2,8,256,1152]{4,3,2,1,0:T(8,128)(2,1)} %bitcast.13, bf16[256,1024]{1,0:T(8,128)(2,1)} %get-tuple-element.37.do_ref, ...), custom_call_target="tpu_custom_call" | custom-call | flops 8000000000 | bytes 41943040 | tf_op jit(solution)/shard_map/grads/pallas_call | solution.py:1035
  287.2 0.0 copy-start
  287.2 1.5 fusion
  288.7 2.3 copy.26
  291.0 1.8 copy.27
  292.8 1.6 copy.28
  294.3 1.9 copy.29
  296.2 0.0 copy-done
  296.2 0.8 copy.30
Async XLA Ops:
  287.2 9.0 %copy-start = (f32[1024,128]{1,0:T(8,128)S(1)}, f32[1024,128]{1,0:T(8,128)}, u32[]{:S(2)}) copy-start(f32[1024,128]{1,0:T(8,128)} %get-tuple-element.75) | copy-start | bytes 1572868

commit v2 on v0

--- a/solution.py
+++ b/solution.py
@@ -3,6 +3,8 @@
 import jax
 import jax.numpy as jnp
 from jax import lax
+from jax.experimental import pallas as pl
+from jax.experimental.pallas import tpu as pltpu
 from jax.sharding import PartitionSpec as P
 
 HEADS = 8
@@ -277,9 +279,858 @@
     )
 
 
+MESH = pl.DeviceIdType.MESH
+BF = jnp.bfloat16
+F32 = jnp.float32
+NEAR_FIRST = ((0, 1, 2, 3), (1, 0, 2, 3), (2, 1, 3, 0), (3, 2, 1, 0))
+FAR_FIRST = ((3, 2, 1, 0), (3, 0, 2, 1), (0, 3, 1, 2), (0, 1, 2, 3))
+
+
+def pick(table, row, column):
+    out = jnp.int32(0)
+    for r, line in enumerate(table):
+        for c, entry in enumerate(line):
+            if entry:
+                out = jnp.where((row == r) & (column == c), entry, out)
+    return out
+
+
+def dot_nn(a, b):
+    return lax.dot_general(a, b, (((1,), (0,)), ((), ())), preferred_element_type=F32)
+
+
+def dot_nt(a, b):
+    return lax.dot_general(a, b, (((1,), (1,)), ((), ())), preferred_element_type=F32)
+
+
+def dot_tn(a, b):
+    return lax.dot_general(a, b, (((0,), (0,)), ((), ())), preferred_element_type=F32)
+
+
+def remote(src, dst, send, recv, **place):
+    return pltpu.make_async_remote_copy(
+        src_ref=src, dst_ref=dst, send_sem=send, recv_sem=recv, device_id=place, device_id_type=MESH
+    )
+
+
+def norm_parts(values):
+    center = values - jnp.mean(values, axis=-1, keepdims=True)
+    spread = jnp.mean(center * center, axis=-1, keepdims=True)
+    inverse = lax.rsqrt(spread + 1e-05)
+    return center * inverse, inverse
+
+
+def greet(q, s, transposed=False):
+    y, c = s // 2, s % 2
+    barrier = pltpu.get_barrier_semaphore()
+
+    def signal(seq, seg):
+        pl.semaphore_signal(barrier, 1, device_id={"seq": seq, "seg": seg}, device_id_type=MESH)
+
+    for d in range(1, 8):
+        for core in range(2):
+            signal(lax.rem(q + d, 8), 2 * y + core)
+    for d in range(1, 4):
+        signal(q, lax.rem(s + d, 4))
+    if transposed:
+        turned = s != q // 2
+
+        @pl.when(turned)
+        def _():
+            signal(2 * s + q % 2, q // 2)
+
+        pl.semaphore_wait(barrier, jnp.where(turned, 18, 17))
+    else:
+        pl.semaphore_wait(barrier, 17)
+
+
+def first_columns(lens, base, rows):
+    place = base + lax.broadcasted_iota(jnp.int32, (rows, 1), 0)
+    start = jnp.zeros((rows, 1), jnp.int32)
+    bound = jnp.zeros((1, 1), jnp.int32)
+    for i in range(lens.shape[0]):
+        bound = bound + lens[i : i + 1, 0:1]
+        start = jnp.where(place >= bound, bound, start)
+    return start
+
+
+def seen_mask(start, base_q, base_k, rows, columns):
+    place = base_q + lax.broadcasted_iota(jnp.int32, (rows, columns), 0)
+    key = base_k + lax.broadcasted_iota(jnp.int32, (rows, columns), 1)
+    return (key <= place) & (key >= start)
+
+
+def rows(k, n):
+    return pl.ds(pl.multiple_of(k * n, n), n)
+
+
+def lanes(k, n=128):
+    return pl.ds(pl.multiple_of(k * n, n), n)
+
+
+T = 256
+
+
+def attend_kernel(
+    x_ref, lens_ref, gain_ref, bias_ref, wq_ref, wo_ref, wu_ref, g_ref,
+    o_ref, wof, wuc, gall, xs, h1, wh, qkv, of, lse, lens,
+    ob, wq_s, wu_v, lens_r, local_sem, qs, qr, ws, wr, xs_send, xs_recv, os_send, os_recv,
+):
+    q, s = lax.axis_index("seq"), lax.axis_index("seg")
+    z, x = q // 2, q % 2
+    y, c = s // 2, s % 2
+    sib = s + 1 - 2 * c
+    across = (1 - y) * 2 + c
+    corner = (1 - y) * 2 + 1 - c
+    head = 2 * z + c
+    home = c == x
+    column = 2 * y + x
+    scale = 1.0 / math.sqrt(HEAD_DIM)
+
+    for j in range(3):
+        at = slice(j * 128, (j + 1) * 128)
+        wh[rows(s, T), at] = wq_ref[:, lanes(8 * j + head)]
+        wq_s[0, :, at] = wq_ref[:, lanes(8 * j + head)]
+        wq_s[1, :, at] = wq_ref[:, lanes(8 * j + 2 * z + 1 - c)]
+
+    @pl.when(home)
+    def _():
+        xs[rows(q, T)] = x_ref[...]
+
+    greet(q, s)
+
+    swap = remote(
+        x_ref, xs.at[rows(q, T)], xs_send.at[12], xs_recv.at[q], seq=2 * z + 1 - x, seg=2 * y + 1 - c
+    )
+
+    @pl.when(jnp.logical_not(home))
+    def _():
+        swap.start()
+
+    mine_wh = wh.at[rows(s, T)]
+    q_across = remote(wq_s.at[0], mine_wh, qs.at[0], qr.at[0], seg=across)
+    q_sib = remote(wq_s.at[1], mine_wh, qs.at[1], qr.at[1], seg=sib)
+    q_corner = remote(wq_s.at[1], mine_wh, qs.at[2], qr.at[2], seg=corner)
+    l_sib = remote(lens_ref, lens_r, qs.at[3], qr.at[3], seg=sib)
+    first = (q_across, q_corner, q_sib, l_sib)
+    for copy in first:
+        copy.start()
+
+    def x_copy(b, k, **to):
+        src = xs.at[rows(b, T)]
+        return remote(src, src, xs_send.at[k], xs_recv.at[b], **to)
+
+    u_across = remote(wu_ref.at[:, lanes(across, 1024)], wuc.at[rows(s, T)], ws.at[0], wr.at[0], seg=across)
+    u_corner = remote(wu_ref.at[:, lanes(corner, 1024)], wuc.at[rows(s, T)], ws.at[1], wr.at[1], seg=corner)
+    u_sib = remote(wu_ref.at[:, lanes(sib, 1024)], wuc.at[rows(s, T)], ws.at[2], wr.at[2], seg=sib)
+    o_across = remote(wo_ref, wof.at[rows(s, T)], ws.at[3], wr.at[3], seg=across)
+    o_sib = remote(wo_ref, wof.at[rows(s, T)], ws.at[4], wr.at[4], seg=sib)
+    o_pass = remote(wof.at[rows(across, T)], wof.at[rows(across, T)], ws.at[5], wr.at[5], seg=sib)
+    g_across = remote(g_ref, gall.at[rows(s, T)], ws.at[6], wr.at[6], seg=across)
+    g_sib = remote(g_ref, gall.at[rows(s, T)], ws.at[7], wr.at[7], seg=sib)
+    g_pass = remote(gall.at[rows(across, T)], gall.at[rows(across, T)], ws.at[8], wr.at[8], seg=sib)
+    own_in = pltpu.make_async_copy(wu_ref.at[:, lanes(s, 1024)], wu_v, local_sem.at[0])
+    own = (
+        pltpu.make_async_copy(wo_ref, wof.at[rows(s, T)], local_sem.at[1]),
+        pltpu.make_async_copy(g_ref, gall.at[rows(s, T)], local_sem.at[2]),
+        pltpu.make_async_copy(wu_v, wuc.at[rows(s, T)], local_sem.at[3]),
+    )
+    for copy in (own_in, u_across, u_corner, o_across, g_across):
+        copy.start()
+    for copy in first:
+        copy.wait_recv()
+    lens[...] = jnp.where(home, lens_ref[...], lens_r[...])
+    own_in.wait()
+    for copy in own:
+        copy.start()
+
+    gain, bias = gain_ref[...], bias_ref[...]
+
+    def project(b):
+        unit, _ = norm_parts(xs[rows(b, T)].astype(F32))
+        low = (unit * gain + bias).astype(BF)
+        h1[rows(b, T)] = low
+        qkv[rows(b, T)] = dot_nn(low, wh[...]).astype(BF)
+
+    def track_step(i, _):
+        zz = pick(NEAR_FIRST, z, i % 4)
+        b = 2 * zz + c
+
+        @pl.when(i < 4)
+        def _():
+            @pl.when((i > 0) | jnp.logical_not(home))
+            def _():
+                x_copy(b, 0, seq=q).wait_recv()
+
+            @pl.when((zz <= z) & (z < 3))
+            def _():
+                x_copy(b, zz, seq=q + 2).start()
+
+            @pl.when((zz >= z) & (z > 0))
+            def _():
+                x_copy(b, 4 + zz, seq=q - 2).start()
+
+            x_copy(b, 8 + zz, seg=sib).start()
+            project(b)
+
+        @pl.when(i > 0)
+        def _():
+            late = 2 * pick(NEAR_FIRST, z, i - 1) + 1 - c
+            x_copy(late, 0, seg=sib).wait_recv()
+            project(late)
+
+        return 0
+
+    lax.fori_loop(0, 5, track_step, 0)
+    for copy in (u_sib, o_sib, g_sib):
+        copy.start()
+
+    def o_copy(i, sender):
+        return remote(
+            ob.at[i], o_ref.at[:, lanes(sender)], os_send.at[i], os_recv.at[sender], seq=i, seg=column
+        )
+
+    mine = pltpu.make_async_copy(ob.at[q], o_ref.at[:, lanes(head)], os_recv.at[head])
+    for i in range(8):
+        n = (i + 1) * T
+        start = first_columns(lens, i * T, T)
+        scores = dot_nt(qkv[i * T : n, :128], qkv[:n, 128:256]) * scale
+        scores = jnp.where(seen_mask(start, i * T, 0, T, n), scores, -1e30)
+        top = jnp.max(scores, axis=1, keepdims=True)
+        weights = jnp.exp(scores - top)
+        total = jnp.sum(weights, axis=1, keepdims=True)
+        mixed = dot_nn(weights.astype(BF), qkv[:n, 256:384]) / total
+        of[i * T : n] = mixed
+        lse[i * T : n] = top + jnp.log(total)
+        ob[i] = mixed.astype(BF)
+        here = (q == i) & home
+
+        @pl.when(jnp.logical_not(here))
+        def _():
+            o_copy(i, head).start()
+
+        @pl.when(here)
+        def _():
+            mine.start()
+
+    o_across.wait_recv()
+    o_pass.start()
+    g_across.wait_recv()
+    g_pass.start()
+
+    def track_end(zz, _):
+        b = 2 * zz + c
+
+        @pl.when((zz <= z) & (z < 3))
+        def _():
+            x_copy(b, zz, seq=q + 2).wait_send()
+
+        @pl.when((zz >= z) & (z > 0))
+        def _():
+            x_copy(b, 4 + zz, seq=q - 2).wait_send()
+
+        x_copy(b, 8 + zz, seg=sib).wait_send()
+        return 0
+
+    lax.fori_loop(0, 4, track_end, 0)
+
+    @pl.when(jnp.logical_not(home))
+    def _():
+        swap.wait_send()
+
+    for i in range(8):
+        @pl.when(jnp.logical_not((q == i) & home))
+        def _():
+            o_copy(i, head).wait_send()
+
+        o_copy(i, i).wait_recv()
+
+    for copy in own:
+        copy.wait()
+    for copy in first + (u_across, u_corner, u_sib, o_across, o_sib, o_pass, g_across, g_sib, g_pass):
+        copy.wait_send()
+    for copy in (u_across, u_corner, u_sib, o_sib, o_pass, g_sib, g_pass):
+        copy.wait_recv()
+
+
+VM = pl.BlockSpec(memory_space=pltpu.VMEM)
+HB = pl.BlockSpec(memory_space=pl.ANY)
+S = jax.ShapeDtypeStruct
+
+
+def attend(x, lens, gain, bias, wq, wo, wu, g):
+    dma = pltpu.SemaphoreType.DMA
+    return pl.pallas_call(
+        attend_kernel,
+        out_shape=(
+            S((256, 1024), BF), S((1024, 1024), BF), S((1024, 1024), BF), S((1024, 1024), BF),
+            S((2048, 1024), BF), S((2048, 1024), BF), S((1024, 384), BF), S((2048, 384), BF),
+            S((2048, 128), F32), S((2048, 1), F32), S((8, 128), jnp.int32),
+        ),
+        in_specs=[VM, VM, VM, VM, VM, VM, HB, VM],
+        out_specs=(VM, HB, HB, HB, VM, VM, VM, VM, VM, VM, VM),
+        scratch_shapes=[
+            pltpu.VMEM((8, 256, 128), BF), pltpu.VMEM((2, 256, 384), BF), pltpu.VMEM((256, 1024), BF),
+            pltpu.VMEM((8, 128), jnp.int32), dma((4,)), dma((4,)), dma((4,)), dma((9,)), dma((9,)),
+            dma((13,)), dma((8,)), dma((8,)), dma((8,)),
+        ],
+        compiler_params=pltpu.CompilerParams(
+            collective_id=0, has_side_effects=True, vmem_limit_bytes=58 * 2**20
+        ),
+        cost_estimate=pl.CostEstimate(flops=5 * 10**9, bytes_accessed=40 * 2**20, transcendentals=2 * 2**20),
+        name="attend",
+    )(x, lens, gain, bias, wq, wo, wu, g)
+
+
+def gelu_parts(u):
+    root = math.sqrt(2.0 / math.pi)
+    square = u * u
+    t = jnp.tanh(root * (u + 0.044715 * (square * u)))
+    value = 0.5 * u * (1.0 + t)
+    slope = 0.5 * (1.0 + t) + 0.5 * u * (1.0 - t * t) * (root * (1.0 + 0.134145 * square))
+    return value, slope
+
+
+def norm_back(grad, gain, unit, inverse):
+    through = grad * gain
+    a = jnp.mean(through, axis=-1, keepdims=True)
+    b = jnp.mean(through * unit, axis=-1, keepdims=True)
+    return inverse * (through - a - unit * b)
+
+
+def ffn_kernel(
+    x_ref, o_ref, g_ref, gain_ref, bias_ref, wo_ref, wu_ref, wd_ref,
+    result_ref, dx_ref, do_ref, sums_ref, pack_ref, outp_ref,
+    h2, za, dua, rp, dp, d_s, d_c, d_p, d_y, r_s, r_c, r_p, r_y, hs, hr, ss, sr,
+):
+    q, s = lax.axis_index("seq"), lax.axis_index("seg")
+    y, c = s // 2, s % 2
+    sib = s + 1 - 2 * c
+    across = (1 - y) * 2 + c
+    corner = (1 - y) * 2 + 1 - c
+
+    barrier = pltpu.get_barrier_semaphore()
+    for d in range(1, 4):
+        pl.semaphore_signal(barrier, 1, device_id={"seg": lax.rem(s + d, 4)}, device_id_type=MESH)
+    pl.semaphore_wait(barrier, 3)
+
+    middle = x_ref[...].astype(F32) + dot_nn(o_ref[...], wo_ref[...])
+    result_f = middle
+    unit, inverse = norm_parts(middle)
+    h2[rows(s, T)] = (unit * gain_ref[...] + bias_ref[...]).astype(BF)
+
+    def h_copy(k, block, to):
+        src = h2.at[rows(block, T)]
+        return remote(src, src, hs.at[k], hr.at[k], seg=to)
+
+    h_across, h_sib, h_pass = h_copy(0, s, across), h_copy(1, s, sib), h_copy(2, across, sib)
+    h_across.start()
+    h_sib.start()
+
+    def work(block):
+        at = rows(block, T)
+        value, slope = gelu_parts(dot_nn(h2[at], wu_ref[...]))
+        za[at] = value.astype(BF)
+        du = (slope * dot_nt(g_ref[at], wd_ref[...])).astype(BF)
+        dua[at] = du
+        dp[block] = dot_nt(du, wu_ref[...])
+        rp[block] = dot_nn(za[at], wd_ref[...])
+
+    work(s)
+    h_sib.wait_recv()
+    work(sib)
+    h_across.wait_recv()
+    h_pass.start()
+    work(across)
+    h_pass.wait_recv()
+    work(corner)
+
+    d_s[0], d_s[1] = dp[corner].astype(BF), dp[sib].astype(BF)
+    r_s[0], r_s[1] = rp[corner].astype(BF), rp[sib].astype(BF)
+    d_core = remote(d_s, d_c, ss.at[0], sr.at[0], seg=sib)
+    r_core = remote(r_s, r_c, ss.at[1], sr.at[1], seg=sib)
+    d_core.start()
+    r_core.start()
+    d_core.wait_recv()
+    d_p[...] = (dp[across] + d_c[0].astype(F32)).astype(BF)
+    d_far = remote(d_p, d_y, ss.at[2], sr.at[2], seg=across)
+    d_far.start()
+    r_core.wait_recv()
+    r_p[...] = (rp[across] + r_c[0].astype(F32)).astype(BF)
+    r_far = remote(r_p, r_y, ss.at[3], sr.at[3], seg=across)
+    r_far.start()
+
+    up = dot_tn(h2[...], dua[...]).astype(BF)
+    for k in range(8):
+        pack_ref[k, :, :512] = up[(k // 2) * T : (k // 2 + 1) * T, (k % 2) * 512 : (k % 2 + 1) * 512]
+    down = dot_tn(za[...], g_ref[...]).astype(BF)
+    for k in range(8):
+        for j in range(4):
+            pack_ref[k, :, 512 + j * 128 : 640 + j * 128] = down[j * T : (j + 1) * T, k * 128 : (k + 1) * 128]
+
+    d_far.wait_recv()
+    grad = dp[s] + d_c[1].astype(F32) + d_y[...].astype(F32)
+    sums_ref[0:1] = jnp.sum(grad * unit, axis=0, keepdims=True)
+    sums_ref[1:2] = jnp.sum(grad, axis=0, keepdims=True)
+    dx = g_ref[rows(s, T)].astype(F32) + norm_back(grad, gain_ref[...], unit, inverse)
+    dx_ref[...] = dx
+    dy = dx.astype(BF)
+    do_ref[...] = dot_nt(dy, wo_ref[...]).astype(BF)
+    out = dot_tn(o_ref[...], dy).astype(BF)
+    for quarter in range(4):
+        for k in range(8):
+            outp_ref[quarter // 2, quarter % 2, k] = out[quarter * T : (quarter + 1) * T, k * 128 : (k + 1) * 128]
+    r_far.wait_recv()
+    result_ref[...] = (result_f + rp[s] + r_c[1].astype(F32) + r_y[...].astype(F32)).astype(BF)
+    for copy in (h_across, h_sib, h_pass, d_core, r_core, d_far, r_far):
+        copy.wait_send()
+
+
+def ffn(x, o, g, gain, bias, wo, wu, wd):
+    dma = pltpu.SemaphoreType.DMA
+    V = pltpu.VMEM
+    block = lambda *lead: V(lead + (256, 1024), BF)
+    return pl.pallas_call(
+        ffn_kernel,
+        out_shape=(
+            S((256, 1024), BF), S((256, 1024), F32), S((256, 1024), BF), S((2, 1024), F32),
+            S((8, 256, 1024), BF), S((2, 2, 8, 256, 128), BF),
+        ),
+        in_specs=[VM] * 8,
+        out_specs=(VM,) * 6,
+        scratch_shapes=[
+            V((1024, 1024), BF), V((1024, 1024), BF), V((1024, 1024), BF), V((4, 256, 1024), F32),
+            V((4, 256, 1024), F32), block(2), block(2), block(), block(), block(2), block(2), block(), block(),
+            dma((3,)), dma((3,)), dma((4,)), dma((4,)),
+        ],
+        compiler_params=pltpu.CompilerParams(
+            collective_id=2, has_side_effects=True, vmem_limit_bytes=60 * 2**20
+        ),
+        cost_estimate=pl.CostEstimate(flops=15 * 10**9, bytes_accessed=40 * 2**20, transcendentals=2**20),
+        name="ffn",
+    )(x, o, g, gain, bias, wo, wu, wd)
+
+
+def grads_kernel(
+    pack_ref, outp_ref, do_ref, dx_ref, sums2_ref, x_ref, xs_ref, h1_ref, wh_ref, qkv_ref, of_ref, lse_ref, lens_ref,
+    gain_ref,
+    dx_out, gqkv_out, gout_out, gup_out, gdown_out, sums_out,
+    x_r, pk, z_r, up_s, up_r, oc_r, oy_r, ox_r, oz_r, doh, dq, dk, dv, dh_s, dhc_r, dhz_r, dht_s, dht_r,
+    gq, gq_b, gq_x, gq_y, gq_s, gq_r, vec, vec_r, xbuf, hbuf,
+    gxs, gxr, gzs, gzr, ups, upr, cs, cr, oxs, oxr, ozs, ozr, dos, dor, dcs, dcr, dzs, dzr, dts, dtr,
+    qs, qr, vs, vr, blk_sem,
+):
+    q, s = lax.axis_index("seq"), lax.axis_index("seg")
+    z, x = q // 2, q % 2
+    y, c = s // 2, s % 2
+    sib = s + 1 - 2 * c
+    across = (1 - y) * 2 + c
+    xq = 2 * z + 1 - x
+    head = 2 * z + c
+    home = c == x
+    column = 2 * y + x
+    away = jnp.logical_not(home)
+    scale = 1.0 / math.sqrt(HEAD_DIM)
+    greet(q, s, True)
+
+    def do_copy(h, block):
+        return remote(
+            do_ref.at[:, h * 128 : (h + 1) * 128], doh.at[rows(block, T)], dos.at[h], dor.at[block],
+            seq=2 * (h // 2) + c, seg=2 * y + h % 2,
+        )
+
+    do_mine = pltpu.make_async_copy(do_ref.at[:, lanes(head)], doh.at[rows(q, T)], dor.at[q])
+    for h in range(8):
+        here = (head == h) & home
+
+        @pl.when(jnp.logical_not(here))
+        def _():
+            do_copy(h, q).start()
+
+        @pl.when(here)
+        def _():
+            do_mine.start()
+
+    def gx_copy(d):
+        return remote(pack_ref.at[2 * d + 1 - x], x_r.at[d], gxs.at[d], gxr.at[d], seq=xq)
+
+    def start_x(j, _):
+        gx_copy(pick(FAR_FIRST, z, j)).start()
+        return 0
+
+    out_core = remote(outp_ref.at[:, 1 - c], oc_r, cs.at[0], cr.at[0], seg=sib)
+    out_core.start()
+    lax.fori_loop(0, 4, start_x, 0)
+    out_core.wait_recv()
+    for part in range(2):
+        oc_r[part] = (oc_r[part].astype(F32) + outp_ref[part, c].astype(F32)).astype(BF)
+    out_y = remote(oc_r.at[1 - y], oy_r, cs.at[1], cr.at[1], seg=across)
+    out_y.start()
+
+    def line_slot(d, place):
+        return jnp.where(d == place, 4, d)
+
+    def line(src, into, send, recv, d):
+        up = remote(src, into.at[d], send.at[d], recv.at[d], seq=q + 2)
+        low = line_slot(d, z - 1)
+        down = remote(src, into.at[low], send.at[d], recv.at[low], seq=q - 2)
+        return up, down
+
+    def come(into, recv, slot):
+        return remote(into.at[slot], into.at[slot], recv.at[slot], recv.at[slot], seq=xq)
+
+    def pass_on(value, keep, into, send, recv, d):
+        has_in = jnp.where(d > z, z > 0, z < 3)
+
+        @pl.when(d != z)
+        def _():
+            @pl.when(has_in)
+            def _():
+                come(into, recv, d).wait_recv()
+                keep[...] = (value() + into[d].astype(F32)).astype(BF)
+
+            @pl.when(jnp.logical_not(has_in))
+            def _():
+                keep[...] = value().astype(BF)
+
+            up, down = line(keep, into, send, recv, d)
+
+            @pl.when(d > z)
+            def _():
+                up.start()
+
+            @pl.when(d < z)
+            def _():
+                down.start()
+
+    def pack_step(j, _):
+        d = pick(FAR_FIRST, z, j)
+        own = 2 * d + x
+        gx_copy(d).wait_recv()
+        pass_on(
+            lambda: pack_ref[own].astype(F32) + x_r[d].astype(F32), pk.at[d], z_r, gzs, gzr, d
+        )
+        return 0
+
+    for b in range(8):
+        do_copy(0, b).wait_recv()
+
+    lax.fori_loop(0, 1, pack_step, 0)
+
+    dk[...] = jnp.zeros_like(dk)
+    dv[...] = jnp.zeros_like(dv)
+    lens = lens_ref[...]
+    for i in range(8):
+        top = i * T
+        start = first_columns(lens, top, T)
+        query = qkv_ref[top : top + T, :128]
+        grad = doh[top : top + T]
+        delta = jnp.sum(grad.astype(F32) * of_ref[top : top + T], axis=1, keepdims=True)
+        log_total = lse_ref[top : top + T]
+        total = jnp.zeros((T, 128), F32)
+        for base in range(0, top + T, 1024):
+            n = min(1024, top + T - base)
+            keys = qkv_ref[base : base + n, 128:256]
+            probs = jnp.exp(dot_nt(query, keys) * scale - log_total)
+            probs = jnp.where(seen_mask(start, top, base, T, n), probs, 0.0)
+            dp = dot_nt(grad, qkv_ref[base : base + n, 256:384])
+            ds = (probs * (dp - delta)).astype(BF)
+            dv[base : base + n] += dot_tn(probs.astype(BF), grad)
+            dk[base : base + n] += dot_tn(ds, query)
+            total += dot_nn(ds, keys)
+        dq[top : top + T] = total
+
+    lax.fori_loop(1, 2, pack_step, 0)
+
+    gq[...] = jnp.zeros_like(gq)
+    vec[...] = jnp.zeros_like(vec)
+    vec[2:4] = sums2_ref[...]
+
+    def block_of(i):
+        return pick(FAR_FIRST, z, i % 4) * 2 + jnp.where(i < 4, 1 - c, c)
+
+    def x_load(i):
+        return pltpu.make_async_copy(xs_ref.at[rows(block_of(i), T)], xbuf.at[i % 2], blk_sem.at[i % 2])
+
+    def h_load(i):
+        return pltpu.make_async_copy(h1_ref.at[rows(block_of(i), T)], hbuf.at[i % 2], blk_sem.at[2 + i % 2])
+
+    def dhc_copy(d):
+        return remote(dh_s.at[2 * d + 1 - c], dhc_r.at[d], dcs.at[d], dcr.at[d], seg=sib)
+
+    x_load(0).start()
+    h_load(0).start()
+
+    def block_step(i, _):
+        b = block_of(i)
+        d = pick(FAR_FIRST, z, i % 4)
+
+        @pl.when(i < 7)
+        def _():
+            x_load(i + 1).start()
+            h_load(i + 1).start()
+
+        at = rows(b, T)
+        low = jnp.concatenate([dq[at] * scale, dk[at] * scale, dv[at]], axis=1).astype(BF)
+        dh = dot_nt(low, wh_ref[...])
+        dh_s[b] = dh.astype(BF)
+
+        @pl.when(i < 4)
+        def _():
+            dhc_copy(d).start()
+
+        @pl.when(i >= 4)
+        def _():
+            dhc_copy(d).wait_recv()
+            pass_on(
+                lambda: dh_s[b].astype(F32) + dhc_r[d].astype(F32), dh_s.at[b], dhz_r, dzs, dzr, d
+            )
+
+        x_load(i).wait()
+        h_load(i).wait()
+        gq[...] += dot_tn(hbuf[i % 2], low)
+        unit, _ = norm_parts(xbuf[i % 2].astype(F32))
+        vec[0:1] += jnp.sum(dh * unit, axis=0, keepdims=True)
+        vec[1:2] += jnp.sum(dh, axis=0, keepdims=True)
+        return 0
+
+    lax.fori_loop(0, 8, block_step, 0)
+
+    gq_b[...] = gq[...].astype(BF).reshape(2, 2, T, 384)
+    q_x = remote(gq_b.at[:, 1 - x], gq_x, qs.at[0], qr.at[0], seq=xq)
+    q_x.start()
+    v_core = remote(vec, vec_r.at[0], vs.at[0], vr.at[0], seg=sib)
+    v_core.start()
+    v_core.wait()
+    vec[...] += vec_r[0]
+    v_y = remote(vec, vec_r.at[1], vs.at[1], vr.at[1], seg=across)
+    v_y.start()
+
+    out_y.wait_recv()
+    oc_r[y] = (oc_r[y].astype(F32) + oy_r[...].astype(F32)).astype(BF)
+
+    def ox_copy(d):
+        return remote(oc_r.at[y, 2 * d + 1 - x], ox_r.at[d], oxs.at[d], oxr.at[d], seq=xq)
+
+    def start_ox(j, _):
+        ox_copy(pick(FAR_FIRST, z, j)).start()
+        return 0
+
+    lax.fori_loop(0, 4, start_ox, 0)
+    v_y.wait()
+    vec[...] += vec_r[1]
+    v_x = remote(vec, vec_r.at[2], vs.at[2], vr.at[2], seq=xq)
+    v_x.start()
+    q_x.wait_recv()
+    for part in range(2):
+        gq_x[part] = (gq_x[part].astype(F32) + gq_b[part, x].astype(F32)).astype(BF)
+    q_y = remote(gq_x.at[1 - y], gq_y, qs.at[1], qr.at[1], seg=across)
+    q_y.start()
+    lax.fori_loop(2, 3, pack_step, 0)
+
+    def out_step(j, _):
+        d = pick(FAR_FIRST, z, j)
+        own = 2 * d + x
+        ox_copy(d).wait_recv()
+        pass_on(
+            lambda: oc_r[y, own].astype(F32) + ox_r[d].astype(F32), oc_r.at[y, own], oz_r, ozs, ozr, d
+        )
+        return 0
+
+    lax.fori_loop(0, 4, out_step, 0)
+    v_x.wait()
+    vec[...] += vec_r[2]
+
+    def v_copy(zz, sender):
+        return remote(vec, vec_r.at[3 + sender], vs.at[3 + zz], vr.at[3 + sender], seq=zz * 2 + x)
+
+    for zz in range(4):
+        @pl.when(zz != z)
+        def _():
+            v_copy(zz, z).start()
+
+    q_y.wait_recv()
+    gq_s[...] = (gq_x[y].astype(F32) + gq_y[...].astype(F32)).astype(BF)
+
+    def column_copy(j):
+        place = 8 * j + head
+        owner, slot = place // 3, place % 3
+        src = gq_s.at[:, j * 128 : (j + 1) * 128]
+        copy = remote(src, gq_r.at[slot], qs.at[2 + j], qr.at[2 + slot], seq=owner, seg=column)
+        local = pltpu.make_async_copy(src, gq_r.at[slot], qr.at[2 + slot])
+        return (owner == q) & home, copy, local
+
+    for j in range(3):
+        here, copy, local = column_copy(j)
+
+        @pl.when(jnp.logical_not(here))
+        def _():
+            copy.start()
+
+        @pl.when(here)
+        def _():
+            local.start()
+
+    lax.fori_loop(3, 4, pack_step, 0)
+
+    def arrived(into, recv):
+        @pl.when(z > 0)
+        def _():
+            come(into, recv, z).wait_recv()
+
+        @pl.when(z == 0)
+        def _():
+            into[0] = jnp.zeros_like(into[0])
+
+        @pl.when(z < 3)
+        def _():
+            come(into, recv, 4).wait_recv()
+
+        @pl.when(z == 3)
+        def _():
+            into[4] = jnp.zeros_like(into[4])
+
+        return into[z].astype(F32) + into[4].astype(F32)
+
+    dht_s[...] = (dh_s[2 * z + c].astype(F32) + dhc_r[z].astype(F32) + arrived(dhz_r, dzr)).astype(BF)
+    turn = remote(dht_s, dht_r, dts, dtr, seq=xq, seg=sib)
+
+    @pl.when(away)
+    def _():
+        turn.start()
+
+    total = pack_ref[q].astype(F32) + x_r[z].astype(F32) + arrived(z_r, gzr)
+    up_s[...] = total[:, :512].astype(BF)
+    turned = s != z
+    up_turn = remote(up_s, up_r, ups, upr, seq=2 * s + x, seg=z)
+    up_own = pltpu.make_async_copy(up_s, up_r, upr)
+
+    @pl.when(turned)
+    def _():
+        up_turn.start()
+
+    @pl.when(jnp.logical_not(turned))
+    def _():
+        up_own.start()
+
+    for j in range(4):
+        gdown_out[j * T : (j + 1) * T] = total[:, 512 + j * 128 : 640 + j * 128]
+    gout_out[...] = oc_r[y, q].astype(F32) + ox_r[z].astype(F32) + arrived(oz_r, ozr)
+    for slot in range(3):
+        come(gq_r, qr.at[pl.ds(2, 3)], slot).wait_recv()
+        gqkv_out[:, slot * 128 : (slot + 1) * 128] = gq_r[slot].astype(F32)
+    vec_r[3 + z] = vec[...]
+    for zz in range(4):
+        @pl.when(zz != z)
+        def _():
+            v_copy(zz, zz).wait_recv()
+
+    sums_out[...] = (vec_r[3] + vec_r[4] + vec_r[5] + vec_r[6])[:4]
+    unit, inverse = norm_parts(x_ref[...].astype(F32))
+
+    @pl.when(away)
+    def _():
+        turn.wait()
+
+    @pl.when(home)
+    def _():
+        dht_r[...] = dht_s[...]
+
+    dx_out[...] = dx_ref[...] + norm_back(dht_r[...].astype(F32), gain_ref[...], unit, inverse)
+    up_own.wait()
+    gup_out[...] = up_r[...].astype(F32)
+
+    for h in range(8):
+        @pl.when(jnp.logical_not((head == h) & home))
+        def _():
+            do_copy(h, q).wait_send()
+
+    def sent(d, _):
+        gx_copy(d).wait_send()
+        ox_copy(d).wait_send()
+        dhc_copy(d).wait_send()
+
+        @pl.when(d != z)
+        def _():
+            line(dh_s.at[d * 2 + c], dhz_r, dzs, dzr, d)[0].wait_send()
+            line(pk.at[d], z_r, gzs, gzr, d)[0].wait_send()
+            line(oc_r.at[y, d * 2 + x], oz_r, ozs, ozr, d)[0].wait_send()
+
+        return 0
+
+    lax.fori_loop(0, 4, sent, 0)
+    for copy in (out_core, out_y, q_x, q_y):
+        copy.wait_send()
+
+    @pl.when(turned)
+    def _():
+        up_turn.wait_send()
+
+    for j in range(3):
+        here, copy, _ = column_copy(j)
+
+        @pl.when(jnp.logical_not(here))
+        def _():
+            copy.wait_send()
+
+    for zz in range(4):
+        @pl.when(zz != z)
+        def _():
+            v_copy(zz, z).wait_send()
+
+
+def grads(pack, outp, do, dx, sums2, x, xs, h1, wh, qkv, of, lse, lens, gain):
+    V = pltpu.VMEM
+    dma = pltpu.SemaphoreType.DMA
+    return pl.pallas_call(
+        grads_kernel,
+        out_shape=(
+            S((256, 1024), F32), S((256, 384), F32), S((256, 128), F32), S((256, 512), F32),
+            S((1024, 128), F32), S((4, 1024), F32),
+        ),
+        in_specs=[VM, VM, VM, VM, VM, VM, HB, HB, VM, VM, VM, VM, VM, VM],
+        out_specs=(VM,) * 6,
+        scratch_shapes=[
+            V((4, 256, 1024), BF), V((4, 256, 1024), BF), V((5, 256, 1024), BF), V((256, 512), BF), V((256, 512), BF),
+            V((2, 8, 256, 128), BF), V((8, 256, 128), BF), V((4, 256, 128), BF), V((5, 256, 128), BF),
+            V((2048, 128), BF), V((2048, 128), F32), V((2048, 128), F32), V((2048, 128), F32),
+            V((8, 256, 1024), BF), V((4, 256, 1024), BF), V((5, 256, 1024), BF), V((256, 1024), BF),
+            V((256, 1024), BF), V((1024, 384), F32), V((2, 2, 256, 384), BF), V((2, 256, 384), BF),
+            V((256, 384), BF), V((256, 384), BF), V((3, 256, 128), BF), V((8, 1024), F32), V((7, 8, 1024), F32),
+            V((2, 256, 1024), BF), V((2, 256, 1024), BF),
+            dma((4,)), dma((4,)), dma((4,)), dma((5,)), dma, dma, dma((2,)), dma((2,)), dma((4,)), dma((4,)),
+            dma((4,)), dma((5,)), dma((8,)), dma((8,)), dma((4,)), dma((4,)), dma((4,)), dma((5,)), dma, dma,
+            dma((5,)), dma((5,)), dma((7,)), dma((7,)), dma((4,)),
+        ],
+        compiler_params=pltpu.CompilerParams(
+            collective_id=1, has_side_effects=True, vmem_limit_bytes=60 * 2**20
+        ),
+        cost_estimate=pl.CostEstimate(flops=8 * 10**9, bytes_accessed=40 * 2**20, transcendentals=2 * 2**20),
+        name="grads",
+    )(pack, outp, do, dx, sums2, x, xs, h1, wh, qkv, of, lse, lens, gain)
+
+
+def per_device_fast(
+    tokens, article_lengths, gain_one, bias_one, w_qkv, w_out, gain_two, bias_two, w_up, w_down, cotangent
+):
+    x = tokens[0]
+    lens = jnp.broadcast_to(article_lengths[0][:, None], (article_lengths.shape[1], 128))
+    o, wo, wu, g, xs, h1, wh, qkv, of, lse, lens = attend(
+        x, lens, gain_one[None], bias_one[None], w_qkv, w_out, w_up, cotangent[0]
+    )
+    result, dx, do, sums2, pack, outp = ffn(
+        x, o, g, gain_two[None], bias_two[None], wo, wu, w_down
+    )
+    dx, gqkv, gout, gup, gdown, sums = grads(
+        pack, outp, do, dx, sums2, x, xs, h1, wh, qkv, of, lse, lens, gain_one[None]
+    )
+    return (result[None], dx[None], sums[0], sums[1], gqkv, gout, sums[2], sums[3], gup, gdown)
+
+
 def solution(mesh):
+    one_pair = mesh.shape["seq"] == HEADS and mesh.shape["seg"] == 4
     return jax.shard_map(
-        per_device,
+        per_device_fast if one_pair else per_device,
         mesh=mesh,
         in_specs=(
             P("seg", "seq", None),

time: 1220 us -> 281 us (0.23)
  the two profiles are of different devices: /device:TPU:4 before, /device:TPU:1 now
where the time goes in v2:
time: 281 us; the launch traced here: 276 us
  Pallas kernels  266 us (95%)
  local copies, waits for them, and re-layouts  8.96 us (3%)
    pallas_call x1, Pallas kernels, grads(): pl.pallas_call(grads_kernel, out_shape=(S((256, 1024), F32), S((256, 384)...  130 us
    pallas_call x1, Pallas kernels, attend(): pl.pallas_call(attend_kernel, out_shape=(S((256, 1024), BF), S((1024, 102...  81.2 us
    pallas_call x1, Pallas kernels, ffn(): pl.pallas_call(ffn_kernel, out_shape=(S((256, 1024), BF), S((256, 1024),...  54.2 us
    unnamed x16, local copies, waits for them, and re-layouts  6.17 us

profile of v2, /device:TPU:1, one launch (start us, length us, event | category | flops | bytes accessed | tf_op | source)
XLA Modules:
  0.0 275.5 jit_solution(16714703417520351004)
XLA Ops:
  0.6 1.3 broadcast_in_dim.27.lens_ref
  2.0 81.2 %attend.1 = (bf16[256,1024]{1,0:T(8,128)(2,1)}, bf16[1024,1024]{1,0:T(8,128)(2,1)}, bf16[1024,1024]{1,0:T(8,128)(2,1)}, bf16[1024,1024]{1,0:T(8,128)(2,1)}, bf16...) custom-call(bf16[256,1024]{1,0:T(8,128)(2,1)} %bitcast.21, ...), custom_call_target="tpu_custom_call" | custom-call | flops 5000000000 | bytes 41943040 | tf_op jit(solution)/shard_map/attend/pallas_call | solution.py:563
  83.2 54.2 %ffn.1 = (bf16[256,1024]{1,0:T(8,128)(2,1)}, f32[256,1024]{1,0:T(8,128)}, bf16[256,1024]{1,0:T(8,128)(2,1)}, f32[2,1024]{1,0:T(2,128)}, bf16[8,256,1024]{2,1,0:T...) custom-call(bf16[256,1024]{1,0:T(8,128)(2,1)} %bitcast.22, bf16[256,1024]{1,0:T(8,128)(2,1)} %get-tuple-element.33.o_ref, ...), custom_call_target="tpu_custom_call" | custom-call | flops 15000000512 | bytes 41943040 | tf_op jit(solution)/shard_map/ffn/pallas_call | solution.py:693
  137.3 0.0 copy-start
  137.4 130.3 %grads.1 = (f32[256,1024]{1,0:T(8,128)}, f32[256,384]{1,0:T(8,128)}, f32[256,128]{1,0:T(8,128)}, f32[256,512]{1,0:T(8,128)}, f32[1024,128]{1,0:T(8,128)}, /*index=5*/f32[4,1024]{1,0:T(4,128)}) custom-call(bf16[8,256,1024]{2,1,0:T(8,128)(2,1)} %get-tuple-element.38.pack_ref, bf16[2,2,8,256,128]{4,3,2,1,0:T(8,128)(2,1)} %get-tuple-element.39.outp_ref, ...), custom_call_target="tpu_custom_call" | custom-call | flops 8000000000 | bytes 41943040 | tf_op jit(solution)/shard_map/grads/pallas_call | solution.py:1085
  267.6 0.0 copy-start.3
  267.7 0.0 copy-start.4
  267.7 1.5 fusion
  269.1 0.0 copy-done
  269.2 0.0 copy-start.2
  269.2 0.8 copy.27
  269.9 0.0 copy-start.1
  270.0 2.4 copy.28
  272.3 0.0 copy-done.3
  272.3 0.7 copy.29
  273.1 0.0 copy-done.4
  273.1 0.7 copy.30
  273.7 0.0 copy-done.2
  273.7 0.8 copy.31
  274.5 0.0 copy-done.1
  274.5 0.8 copy.32
Async XLA Ops:
  137.3 131.8 %copy-start = (bf16[256,1024]{1,0:T(8,128)(2,1)S(1)}, bf16[256,1024]{1,0:T(8,128)(2,1)}, u32[]{:S(2)}) copy-start(bf16[256,1024]{1,0:T(8,128)(2,1)} %get-tuple-element.37) | copy-start | bytes 1572868
  267.6 4.7 %copy-start.3 = (f32[256,384]{1,0:T(8,128)S(1)}, f32[256,384]{1,0:T(8,128)}, u32[]{:S(2)}) copy-start(f32[256,384]{1,0:T(8,128)} %get-tuple-element.74) | copy-start | bytes 1179652
  267.7 5.4 %copy-start.4 = (f32[256,128]{1,0:T(8,128)S(1)}, f32[256,128]{1,0:T(8,128)}, u32[]{:S(2)}) copy-start(f32[256,128]{1,0:T(8,128)} %get-tuple-element.75) | copy-start | bytes 393220
  269.2 4.6 %copy-start.2 = (f32[256,512]{1,0:T(8,128)S(1)}, f32[256,512]{1,0:T(8,128)}, u32[]{:S(2)}) copy-start(f32[256,512]{1,0:T(8,128)} %get-tuple-element.78) | copy-start | bytes 1572868
  269.9 4.6 %copy-start.1 = (f32[1024,128]{1,0:T(8,128)S(1)}, f32[1024,128]{1,0:T(8,128)}, u32[]{:S(2)}) copy-start(f32[1024,128]{1,0:T(8,128)} %get-tuple-element.79) | copy-start | bytes 1572868
